TPU v7x, 512 devices: a whole 4x4x16 slice. The times are simulated.
512 devices in a mesh: row: 32 (over y, z_hi, core), col: 16 (over z_lo, x).
Axes of the slice: x: 4, y: 4, z: 16 (z_hi: 4, z_lo: 4; z = z_hi * 4 + z_lo), core: 2. Of those that a mesh axis runs over, the one named last changes fastest.
Arguments:
- pair: bfloat16 [2048, 2048, 128], P('row', 'col'), may hold values from -6 to 6
- atoms: bfloat16 [32768, 128], P(('row', 'col')), may hold values from -6 to 6
- atom_token: int32 [32768], P(('row', 'col')), may hold values from 0 to 2047, as said below
- atom_mask: int32 [32768], P(('row', 'col')), may hold values from 0 to 1, as said below
- bias_gain: float32 [128], replicated, may hold values from 0.5 to 1.5
- w_pair_bias: bfloat16 [128, 4], replicated, may hold values from -0.75 to 0.75
- trans_gain: float32 [128], replicated, may hold values from 0.5 to 1.5
- w_pair_up: bfloat16 [128, 1024], replicated, may hold values from -0.5 to 0.5
- w_pair_down: bfloat16 [512, 128], replicated, may hold values from -0.25 to 0.25
- atom_gain: float32 [128], replicated, may hold values from 0.5 to 1.5
- w_query: bfloat16 [128, 128], replicated
- w_key: bfloat16 [128, 128], replicated
- w_value: bfloat16 [128, 128], replicated, may hold values from -0.5 to 0.5
- w_gate: bfloat16 [128, 128], replicated, may hold values from -1 to 1
- w_out: bfloat16 [128, 128], replicated, may hold values from -0.75 to 0.75
- mid_gain: float32 [128], replicated, may hold values from 0.5 to 1.5
- w_atom_up: bfloat16 [128, 512], replicated, may hold values from -0.5 to 0.5
- w_atom_down: bfloat16 [256, 128], replicated, may hold values from -0.5 to 0.5
- w_single: bfloat16 [128, 384], replicated, may hold values from -0.5 to 0.5
- w_outer_row: bfloat16 [384, 128], replicated, may hold values from -0.4375 to 0.4375
- w_outer_col: bfloat16 [384, 128], replicated, may hold values from -0.4375 to 0.4375
Outputs:
- atoms_out: bfloat16 [32768, 128], P(('row', 'col'))
- pair_out: bfloat16 [2048, 2048, 128], P('row', 'col')
Inputs may be any that keep to these rules, and one draw needn't show every extreme that they name: `atom_token`: the atoms of block j (atoms j * 64 to (j + 1) * 64 - 1) name only tokens j * 4 to (j + 1) * 4 - 1, so no token is shared between blocks; along a block the token numbers never decrease; every token has at least one atom with mask 1. `atom_mask`: within each block of 64 atoms the ones come first, at least 48 of them.
All inputs are finite; a program needn't handle non-finite values.
Results may differ from a plain program's by a relative error of at most 0.0074.
Values may be sent and summed in bfloat16 or wider, within the bound.
No kernel may reach another device: no remote copies, remote signals or barrier semaphores. Data moves between devices by JAX's collectives and lax.ppermute only.
A program may use at most 64 MiB of HBM per device.

v0:
```python
import math

import jax
import jax.numpy as jnp
from jax import lax
from jax.sharding import PartitionSpec as P

QW = 32
KW = 128


def with_halo(cells, sides, width):
    for axis, dim in sides:
        count = lax.axis_size(axis)
        ends = count - 1
        head = lax.slice_in_dim(cells, 0, width, axis=dim)
        tail = lax.slice_in_dim(cells, cells.shape[dim] - width, cells.shape[dim], axis=dim)
        cells = jnp.concatenate(
            [
                lax.ppermute(tail, axis, [(i, (i + 1) % count) for i in range(ends)]),
                cells,
                lax.ppermute(head, axis, [((i + 1) % count, i) for i in range(ends)]),
            ],
            axis=dim,
        )
    return cells


def layer_norm(values):
    mean = jnp.mean(values, axis=-1, keepdims=True)
    centred = values - mean
    var = jnp.mean(centred * centred, axis=-1, keepdims=True)
    return centred * lax.rsqrt(var + 1e-05)


def body(
    pair,
    atoms,
    atom_token,
    atom_mask,
    bias_gain,
    w_pair_bias,
    trans_gain,
    w_pair_up,
    w_pair_down,
    atom_gain,
    w_query,
    w_key,
    w_value,
    w_gate,
    w_out,
    mid_gain,
    w_atom_up,
    w_atom_down,
    w_single,
    w_outer_row,
    w_outer_col,
):
    tok_rows, tok_cols, chans = pair.shape
    heads = w_pair_bias.shape[1]
    per_block, width = atoms.shape
    head_dim = width // heads
    hidden_pair = w_pair_down.shape[0]
    hidden_atom = w_atom_down.shape[0]
    share = tok_rows // lax.axis_size("col")
    block_index = lax.axis_index(("row", "col"))
    col_index = lax.axis_index("col")
    step = math.gcd(tok_rows, max(1, 1024 // tok_cols))
    count = tok_rows // step
    pair_blocks = pair.reshape(count, step, tok_cols, chans)

    def first_pass(block):
        normed = layer_norm(block.astype(jnp.float32))
        normed_bias = (normed * bias_gain).astype(jnp.bfloat16)
        normed_trans = (normed * trans_gain).astype(jnp.bfloat16)
        table = jnp.einsum(
            "tuc,ch->htu", normed_bias, w_pair_bias, preferred_element_type=jnp.float32
        ).astype(jnp.bfloat16)
        return (table, normed_trans)

    tables, normed_trans = lax.map(first_pass, pair_blocks)
    bias_table = jnp.transpose(tables, (1, 0, 2, 3)).reshape(heads, tok_rows, tok_cols)
    whole = lax.all_gather(bias_table, "col", axis=2, tiled=True)
    own_rows = lax.dynamic_slice_in_dim(whole, col_index * share, share, 1)
    widened = jnp.pad(own_rows, ((0, 0), (0, 0), (share, share)))
    band = lax.dynamic_slice_in_dim(widened, block_index * share, 3 * share, 2)
    atom_norm = (layer_norm(atoms.astype(jnp.float32)) * atom_gain).astype(jnp.bfloat16)
    query = jnp.dot(atom_norm, w_query, preferred_element_type=jnp.float32).astype(jnp.bfloat16)
    key = jnp.dot(atom_norm, w_key, preferred_element_type=jnp.float32).astype(jnp.bfloat16)
    value = jnp.dot(atom_norm, w_value, preferred_element_type=jnp.float32).astype(jnp.bfloat16)
    gate_lin = jnp.dot(atom_norm, w_gate, preferred_element_type=jnp.float32)
    local_token = atom_token - block_index * share
    key_value = jnp.concatenate([key, value], axis=1)
    rim_token = local_token.astype(jnp.bfloat16)
    rim_mask = atom_mask.astype(jnp.bfloat16)
    rim = (KW - QW) // 2
    ext_kv, ext_token, ext_mask = (
        with_halo(key_value, ((("row", "col"), 0),), rim),
        with_halo(rim_token, ((("row", "col"), 0),), rim),
        with_halo(rim_mask, ((("row", "col"), 0),), rim),
    )
    spots = jnp.arange(ext_kv.shape[0], dtype=jnp.int32)
    key_token = (
        ext_token.astype(jnp.int32)
        + share * (spots >= rim).astype(jnp.int32)
        + share * (spots >= rim + per_block).astype(jnp.int32)
    )
    query_onehot = (local_token[:, None] == jnp.arange(share, dtype=jnp.int32)[None, :]).astype(
        jnp.bfloat16
    )
    key_onehot = (key_token[:, None] == jnp.arange(3 * share, dtype=jnp.int32)[None, :]).astype(
        jnp.bfloat16
    )
    query_band = jnp.einsum(
        "qa,hab->hqb", query_onehot, band, preferred_element_type=jnp.float32
    ).astype(jnp.bfloat16)
    atom_bias = jnp.einsum(
        "hqb,kb->hqk", query_band, key_onehot, preferred_element_type=jnp.float32
    )
    windows = per_block // QW
    query_win = query.reshape(windows, QW, heads, head_dim)
    key_win = jnp.stack([ext_kv[w * QW : w * QW + KW, :width] for w in range(windows)]).reshape(
        windows, KW, heads, head_dim
    )
    value_win = jnp.stack([ext_kv[w * QW : w * QW + KW, width:] for w in range(windows)]).reshape(
        windows, KW, heads, head_dim
    )
    bias_win = jnp.stack(
        [atom_bias[:, w * QW : (w + 1) * QW, w * QW : w * QW + KW] for w in range(windows)]
    )
    valid_win = jnp.stack([ext_mask[w * QW : w * QW + KW] > 0.5 for w in range(windows)])
    logits = (
        jnp.einsum("wqhd,wkhd->whqk", query_win, key_win, preferred_element_type=jnp.float32)
        * (1.0 / head_dim**0.5)
        + bias_win
    )
    logits = jnp.where(valid_win[:, None, None, :], logits, -1000000000.0)
    top = jnp.max(logits, axis=-1, keepdims=True)
    expo = jnp.exp(logits - top)
    weights = (expo / jnp.sum(expo, axis=-1, keepdims=True)).astype(jnp.bfloat16)
    attended = jnp.einsum(
        "whqk,wkhd->wqhd", weights, value_win, preferred_element_type=jnp.float32
    ).reshape(per_block, width)
    gated = (attended * jax.nn.sigmoid(gate_lin)).astype(jnp.bfloat16)
    atoms_mid = atoms.astype(jnp.float32) + jnp.dot(
        gated, w_out, preferred_element_type=jnp.float32
    )
    mid_norm = (layer_norm(atoms_mid) * mid_gain).astype(jnp.bfloat16)
    gate_up = jnp.dot(mid_norm, w_atom_up, preferred_element_type=jnp.float32)
    atom_hidden = (jax.nn.silu(gate_up[:, :hidden_atom]) * gate_up[:, hidden_atom:]).astype(
        jnp.bfloat16
    )
    atoms_out = (
        atoms_mid + jnp.dot(atom_hidden, w_atom_down, preferred_element_type=jnp.float32)
    ).astype(jnp.bfloat16)
    single_terms = jax.nn.relu(jnp.dot(atoms_out, w_single, preferred_element_type=jnp.float32))
    live_onehot = query_onehot.astype(jnp.float32) * atom_mask.astype(jnp.float32)[:, None]
    sums = jnp.dot(live_onehot.T, single_terms, precision=lax.Precision.HIGHEST)
    counts = jnp.sum(live_onehot, axis=0)
    singles = (sums / counts[:, None]).astype(jnp.bfloat16)
    row_terms = jnp.dot(singles, w_outer_row, preferred_element_type=jnp.float32).astype(
        jnp.bfloat16
    )
    col_terms = jnp.dot(singles, w_outer_col, preferred_element_type=jnp.float32).astype(
        jnp.bfloat16
    )
    row_block, col_block = (
        lax.all_gather(row_terms, "col", axis=0, tiled=True),
        lax.all_gather(col_terms, "col", axis=0, tiled=True),
    )
    every = lax.all_gather(col_block, "row", axis=0, tiled=True)
    col_part = lax.dynamic_slice_in_dim(every, col_index * tok_cols, tok_cols, 0)
    col_float = col_part.astype(jnp.float32)

    def second_pass(items):
        block, normed, row_part = items
        pair_gu = jnp.dot(normed.reshape(-1, chans), w_pair_up, preferred_element_type=jnp.float32)
        pair_hidden = (jax.nn.silu(pair_gu[:, :hidden_pair]) * pair_gu[:, hidden_pair:]).astype(
            jnp.bfloat16
        )
        pair_update = jnp.dot(pair_hidden, w_pair_down, preferred_element_type=jnp.float32).reshape(
            block.shape
        )
        total = (
            block.astype(jnp.float32)
            + pair_update
            + row_part.astype(jnp.float32)[:, None, :]
            + col_float[None, :, :]
        )
        return total.astype(jnp.bfloat16)

    pair_out = lax.map(
        second_pass, (pair_blocks, normed_trans, row_block.reshape(count, step, chans))
    )
    return (atoms_out, pair_out.reshape(tok_rows, tok_cols, chans))


def solution(mesh):
    in_specs = (
        P("row", "col", None),
        P(("row", "col"), None),
        P(("row", "col")),
        P(("row", "col")),
        P(),
        P(),
        P(),
        P(),
        P(),
        P(),
        P(),
        P(),
        P(),
        P(),
        P(),
        P(),
        P(),
        P(),
        P(),
        P(),
        P(),
    )
    out_specs = (P(("row", "col"), None), P("row", "col", None))
    return jax.shard_map(body, mesh=mesh, in_specs=in_specs, out_specs=out_specs, check_vma=False)
```

profile of v0, /device:TPU:2, one launch (start us, length us, event | category | flops | bytes accessed | tf_op | source)
XLA Modules:
  0.0 283.3 jit_solution(16429221955388754528)
XLA Ops:
  8.2 3.4 %collective-permute-start.4 = (bf16[48]{0:T(256)(128)(2,1)S(1)}, bf16[48]{0:T(256)(128)(2,1)S(1)}, u32[]{:S(2)}, u32[]{:S(2)}) collective-permute-start(bf16[48]{0:T(256)(128)(2,1)S(1)} %get-tuple-element.131), channel_id=1, source_target_pairs={{0,1},{1,2},{2,3},{3,4},{4,5},{5,6},{6,7},{7,8},{8,9},{9,10},{10,1... | collective-permute-start | bytes 296 | tf_op jit(solution)/shard_map/ppermute | solution.py:20
  11.5 5.7 %collective-permute-start.5 = (bf16[48]{0:T(256)(128)(2,1)S(1)}, bf16[48]{0:T(256)(128)(2,1)S(1)}, u32[]{:S(2)}, u32[]{:S(2)}) collective-permute-start(bf16[48]{0:T(256)(128)(2,1)S(1)} %get-tuple-element.132), channel_id=1, source_target_pairs={{1,0},{2,1},{3,2},{4,3},{5,4},{6,5},{7,6},{8,7},{9,8},{10,9},{11,1... | collective-permute-start | bytes 296 | tf_op jit(solution)/shard_map/ppermute | solution.py:22
  17.3 1.8 broadcast.128.clone
  19.2 16.5 %while.22 = (s32[]{:T(128)}, bf16[8,4,8,128]{3,1,2,0:T(4,128)(2,1)S(1)}, bf16[8,8,128,128]{3,2,1,0:T(8,128)(2,1)}, bf16[8,8,128,128]{3,2,1,0:T(8,128)(2,1)S(1)},...) while((s32[]{:T(128)}, bf16[8,4,8,128]{3,1,2,0:T(4,128)(2,1)S(1)}, ...), condition=%wide.region_5.6_spmd, body=%wide.region_2.5_spmd.sunk | while | flops 3150850 | bytes 1367645 | solution.py:81
  19.8 1.1 fusion.148
  21.8 1.0 fusion.148
  23.9 1.0 fusion.148
  26.0 1.0 fusion.148
  28.0 1.1 fusion.148
  30.1 1.0 fusion.148
  32.1 1.0 fusion.148
  34.2 1.1 fusion.148
  37.2 1.9 collective-permute-start
  39.2 1.9 collective-permute-start.2
  41.1 3.9 %collective-permute-start.3 = (bf16[48]{0:T(256)(128)(2,1)S(1)}, bf16[48]{0:T(256)(128)(2,1)S(1)}, u32[]{:S(2)}, u32[]{:S(2)}) collective-permute-start(bf16[48]{0:T(256)(128)(2,1)S(1)} %get-tuple-element.130), channel_id=1, source_target_pairs={{1,0},{2,1},{3,2},{4,3},{5,4},{6,5},{7,6},{8,7},{9,8},{10,9},{11,1... | collective-permute-start | bytes 296 | tf_op jit(solution)/shard_map/ppermute | solution.py:22
  45.5 1.9 collective-permute-start.1
  48.1 3.1 %collective-permute-done.1 = bf16[48,256]{1,0:T(8,128)(2,1)S(1)} collective-permute-done((bf16[48,256]{1,0:T(8,128)(2,1)S(1)}, bf16[48,256]{1,0:T(8,128)(2,1)S(1)}, u32[]{:S(2)}, u32[]{:S(2)}) %collective-permute-start.1) | collective-permute-done | bytes 24608 | tf_op jit(solution)/shard_map/ppermute | solution.py:22
  51.7 59.3 %all-gather.4.cloned.1.call-done = bf16[4,64,2048]{2,1,0:T(8,128)(2,1)} async-done(((bf16[4,64,128]{2,1,0:T(8,128)(2,1)}), bf16[4,64,2048]{2,1,0:T(8,128)(2,1)}) %all-gather.4.cloned.1.call-update) | async-done | bytes 1048592 | tf_op jit(solution)/shard_map/all_gather | solution.py:83
  115.4 37.6 %all-gather.1 = bf16[16,4,128]{2,1,0:T(4,128)(2,1)S(1)} all-gather(bf16[1,4,128]{2,1,0:T(4,128)(2,1)S(1)} %fusion.39), channel_id=1, replica_groups=mesh['row'=32,'col'=16] {'col'}, dimensions={0}, use_global_device_ids=true | all-gather | bytes 17408 | tf_op jit(solution)/shard_map/all_gather | solution.py:169
  153.0 54.0 %all_gather.15 = bf16[2048,128]{1,0:T(8,128)(2,1)S(1)} all-gather(bf16[64,128]{1,0:T(8,128)(2,1)S(1)} %bitcast.108), channel_id=1, replica_groups=mesh['row'=32,'col'=16] {'row'}, dimensions={0}, use_global_device_ids=true | all-gather | bytes 540672 | tf_op jit(solution)/shard_map/all_gather | solution.py:171
  207.2 41.9 %all-gather = bf16[16,4,128]{2,1,0:T(4,128)(2,1)S(1)} all-gather(bf16[1,4,128]{2,1,0:T(4,128)(2,1)S(1)} %fusion.38), channel_id=1, replica_groups=mesh['row'=32,'col'=16] {'col'}, dimensions={0}, use_global_device_ids=true | all-gather | bytes 17408 | tf_op jit(solution)/shard_map/all_gather | solution.py:168
  249.1 1.8 broadcast.128
  250.9 25.5 %while.23 = (s32[]{:T(128)}, bf16[8,8,128,128]{3,2,1,0:T(8,128)(2,1)}, bf16[8,8,128,128]{3,2,1,0:T(8,128)(2,1)S(1)}, bf16[8,8,128,128]{3,2,1,0:T(8,128)(2,1)}, b...) while((s32[]{:T(128)}, ...), condition=%wide.region_12.13_spmd, body=%wide.region_11.12_spmd.sunk | while | flops 406455296 | bytes 11217509 | solution.py:192
  250.9 1.0 constant_dynamic-slice_fusion.3
  (173 shorter events, 40.6 us)
Async XLA Ops:
  7.2 107.3 %copy-start = (bf16[128,512]{1,0:T(8,128)(2,1)S(1)}, bf16[128,512]{1,0:T(8,128)(2,1)}, u32[]{:S(2)}) copy-start(bf16[128,512]{1,0:T(8,128)(2,1)} %param.41) | copy-start | bytes 393220
  7.2 103.8 %all-gather.4.cloned.1.call-start = ((), (), s32[]{:S(2)}) async-start(), calls=%async_computation | async-start | bytes 1114112 | tf_op jit(solution)/shard_map/all_gather | solution.py:83
  8.2 39.8 %collective-permute-start.4 = (bf16[48]{0:T(256)(128)(2,1)S(1)}, bf16[48]{0:T(256)(128)(2,1)S(1)}, u32[]{:S(2)}, u32[]{:S(2)}) collective-permute-start(bf16[48]{0:T(256)(128)(2,1)S(1)} %get-tuple-element.131), channel_id=1, source_target_pairs={{0,1},{1,2},{2,3},{3,4},{4,5},{5,6},{6,7},{7,8},{8,9},{9,10},{10,1... | collective-permute-start | bytes 296 | tf_op jit(solution)/shard_map/ppermute | solution.py:20
  11.5 36.4 %collective-permute-start.5 = (bf16[48]{0:T(256)(128)(2,1)S(1)}, bf16[48]{0:T(256)(128)(2,1)S(1)}, u32[]{:S(2)}, u32[]{:S(2)}) collective-permute-start(bf16[48]{0:T(256)(128)(2,1)S(1)} %get-tuple-element.132), channel_id=1, source_target_pairs={{1,0},{2,1},{3,2},{4,3},{5,4},{6,5},{7,6},{8,7},{9,8},{10,9},{11,1... | collective-permute-start | bytes 296 | tf_op jit(solution)/shard_map/ppermute | solution.py:22
  19.1 17.3 %copy-start.6 = (bf16[64,128]{1,0:T(8,128)(2,1)S(1)}, bf16[64,128]{1,0:T(8,128)(2,1)}, u32[]{:S(2)}) copy-start(bf16[64,128]{1,0:T(8,128)(2,1)} %param.26) | copy-start | bytes 49156
  19.1 17.6 %copy-start.12 = (bf16[128,128]{1,0:T(8,128)(2,1)S(1)}, bf16[128,128]{1,0:T(8,128)(2,1)}, u32[]{:S(2)}) copy-start(bf16[128,128]{1,0:T(8,128)(2,1)} %param.37) | copy-start | bytes 98308
  19.1 17.6 %copy-start.20 = (f32[128]{0:T(128)S(1)}, f32[128]{0:T(128)}, u32[]{:S(2)}) copy-start(f32[128]{0:T(128)} %param.34) | copy-start | bytes 1540
  19.2 17.8 %copy-start.13 = (bf16[128,128]{1,0:T(8,128)(2,1)S(1)}, bf16[128,128]{1,0:T(8,128)(2,1)}, u32[]{:S(2)}) copy-start(bf16[128,128]{1,0:T(8,128)(2,1)} %param.36) | copy-start | bytes 98308
  19.2 19.9 %copy-start.19 = (s32[64]{0:T(128)S(1)}, s32[64]{0:T(128)}, u32[]{:S(2)}) copy-start(s32[64]{0:T(128)} %param.28) | copy-start | bytes 772
  19.2 25.9 %copy-start.14 = (bf16[128,128]{1,0:T(8,128)(2,1)S(1)}, bf16[128,128]{1,0:T(8,128)(2,1)}, u32[]{:S(2)}) copy-start(bf16[128,128]{1,0:T(8,128)(2,1)} %param.35) | copy-start | bytes 98308
  36.4 77.4 %copy-start.15 = (bf16[128,128]{1,0:T(8,128)(2,1)S(1)}, bf16[128,128]{1,0:T(8,128)(2,1)}, u32[]{:S(2)}) copy-start(bf16[128,128]{1,0:T(8,128)(2,1)} %param.39) | copy-start | bytes 98308
  36.4 77.5 %copy-start.16 = (bf16[128,128]{1,0:T(8,128)(2,1)S(1)}, bf16[128,128]{1,0:T(8,128)(2,1)}, u32[]{:S(2)}) copy-start(bf16[128,128]{1,0:T(8,128)(2,1)} %param.38) | copy-start | bytes 98308
  36.9 77.6 %copy-start.9 = (f32[128]{0:T(128)S(1)}, f32[128]{0:T(128)}, u32[]{:S(2)}) copy-start(f32[128]{0:T(128)} %param.40) | copy-start | bytes 1540
  37.2 11.0 %collective-permute-start = (bf16[48,256]{1,0:T(8,128)(2,1)S(1)}, bf16[48,256]{1,0:T(8,128)(2,1)S(1)}, u32[]{:S(2)}, u32[]{:S(2)}) collective-permute-start(bf16[48,256]{1,0:T(8,128)(2,1)S(1)} %get-tuple-element.123), channel_id=1, source_target_pairs={{0,1},{1,2},{2,3},{3,4},{4,5},{5,6},{6,7},{7,8},{8,9},{9,10},{10,1... | collective-permute-start | bytes 73736 | tf_op jit(solution)/shard_map/ppermute | solution.py:20
  39.2 6.3 %collective-permute-start.2 = (bf16[48]{0:T(256)(128)(2,1)S(1)}, bf16[48]{0:T(256)(128)(2,1)S(1)}, u32[]{:S(2)}, u32[]{:S(2)}) collective-permute-start(bf16[48]{0:T(256)(128)(2,1)S(1)} %get-tuple-element.129), channel_id=1, source_target_pairs={{0,1},{1,2},{2,3},{3,4},{4,5},{5,6},{6,7},{7,8},{8,9},{9,10},{10,1... | collective-permute-start | bytes 296 | tf_op jit(solution)/shard_map/ppermute | solution.py:20
  41.1 6.8 %collective-permute-start.3 = (bf16[48]{0:T(256)(128)(2,1)S(1)}, bf16[48]{0:T(256)(128)(2,1)S(1)}, u32[]{:S(2)}, u32[]{:S(2)}) collective-permute-start(bf16[48]{0:T(256)(128)(2,1)S(1)} %get-tuple-element.130), channel_id=1, source_target_pairs={{1,0},{2,1},{3,2},{4,3},{5,4},{6,5},{7,6},{8,7},{9,8},{10,9},{11,1... | collective-permute-start | bytes 296 | tf_op jit(solution)/shard_map/ppermute | solution.py:22
  45.3 69.5 %copy-start.11 = (bf16[256,128]{1,0:T(8,128)(2,1)S(1)}, bf16[256,128]{1,0:T(8,128)(2,1)}, u32[]{:S(2)}) copy-start(bf16[256,128]{1,0:T(8,128)(2,1)} %param.42) | copy-start | bytes 196612
  45.5 5.7 %collective-permute-start.1 = (bf16[48,256]{1,0:T(8,128)(2,1)S(1)}, bf16[48,256]{1,0:T(8,128)(2,1)S(1)}, u32[]{:S(2)}, u32[]{:S(2)}) collective-permute-start(bf16[48,256]{1,0:T(8,128)(2,1)S(1)} %get-tuple-element.124), channel_id=1, source_target_pairs={{1,0},{2,1},{3,2},{4,3},{5,4},{6,5},{7,6},{8,7},{9,8},{10,9},{11,1... | collective-permute-start | bytes 73736 | tf_op jit(solution)/shard_map/ppermute | solution.py:22
  51.2 63.7 %copy-start.5 = (bf16[128,384]{1,0:T(8,128)(2,1)S(1)}, bf16[128,384]{1,0:T(8,128)(2,1)}, u32[]{:S(2)}) copy-start(bf16[128,384]{1,0:T(8,128)(2,1)} %param.43) | copy-start | bytes 294916
  51.5 63.7 %copy-start.3 = (bf16[384,128]{1,0:T(8,128)(2,1)S(1)}, bf16[384,128]{1,0:T(8,128)(2,1)}, u32[]{:S(2)}) copy-start(bf16[384,128]{1,0:T(8,128)(2,1)} %param.45) | copy-start | bytes 294916
  112.5 94.5 %copy-start.4 = (bf16[384,128]{1,0:T(8,128)(2,1)S(1)}, bf16[384,128]{1,0:T(8,128)(2,1)}, u32[]{:S(2)}) copy-start(bf16[384,128]{1,0:T(8,128)(2,1)} %param.44) | copy-start | bytes 294916
  113.8 137.1 %copy-start.2 = (bf16[128,1024]{1,0:T(8,128)(2,1)S(1)}, bf16[128,1024]{1,0:T(8,128)(2,1)}, u32[]{:S(2)}) copy-start(bf16[128,1024]{1,0:T(8,128)(2,1)} %param.32) | copy-start | bytes 786436
  113.8 137.1 %copy-start.10 = (bf16[512,128]{1,0:T(8,128)(2,1)S(1)}, bf16[512,128]{1,0:T(8,128)(2,1)}, u32[]{:S(2)}) copy-start(bf16[512,128]{1,0:T(8,128)(2,1)} %param.33) | copy-start | bytes 393220
  114.9 136.0 %copy-start.7 = (bf16[64,128]{1,0:T(8,128)(2,1)}, bf16[64,128]{1,0:T(8,128)(2,1)S(1)}, u32[]{:S(2)}) copy-start(bf16[64,128]{1,0:T(8,128)(2,1)S(1)} %fusion.34) | copy-start | bytes 49156
  (4 other events, 47.7 us)
Sparse Core Ops, SparseCore 0:
  36.5 74.4 all-gather.3
where the time goes:
time: 284 us; the launch traced here: 283 us
  blocking collectives  134 us (47%)
  waiting for transfers between devices  62.9 us (22%)
  other arithmetic  20.8 us (7%)
  starting transfers between devices  18.8 us (7%)
  matrix products  18.2 us (6%)
  between operations  14.5 us (5%)
  local copies, waits for them, and re-layouts  14.2 us (5%)
    all_gather x1, waiting for transfers between devices, body(): whole = lax.all_gather(bias_table, 'col', axis=2, tiled=True)  59.3 us
    all_gather x1, blocking collectives, body(): every = lax.all_gather(col_block, 'row', axis=0, tiled=True)  54 us
    all_gather x1, blocking collectives, body(): lax.all_gather(row_terms, 'col', axis=0, tiled=True)  41.9 us
    all_gather x1, blocking collectives, body(): lax.all_gather(col_terms, 'col', axis=0, tiled=True)  37.6 us
    dynamic_update_slice x16, other arithmetic, body(): tables, normed_trans = lax.map(first_pass, pair_blocks)  14.8 us
    ppermute x3, starting transfers between devices, with_halo(): lax.ppermute(head, axis, [((i + 1) % count, i) for i in range(ends)])  11.5 us
    dynamic_slice x8, local copies, waits for them, and re-layouts, body(): tables, normed_trans = lax.map(first_pass, pair_blocks)  7.74 us
    ppermute x3, starting transfers between devices, with_halo(): lax.ppermute(tail, axis, [(i, (i + 1) % count) for i in range(ends)])  7.22 us
  transfers between devices with their start and end apart: 7, of which 3 were waited for; matrix products, arithmetic and copies ran while one was open for 7% of the time, Pallas kernels for 0%

commit v1 on v0

v1 whole, which is shorter than its diff:
```python
import functools

import jax
import jax.numpy as jnp
from jax import lax
from jax.experimental import pallas as pl
from jax.experimental.pallas import tpu as pltpu
from jax.sharding import PartitionSpec as P

F32 = jnp.float32
BF16 = jnp.bfloat16
N4 = 4
QW = 32
KW = 128
RIM = (KW - QW) // 2
ATOMS = 64
EXT = ATOMS + 2 * RIM
HEADS = 4
HEAD = 32
PACK = 80
FAR = -3.0e38
SPLIT = 40
PAIR_ROWS = 8


def rank(y, zh, core, zl, x):
    return ((y * N4 + zh) * 2 + core) * 16 + zl * N4 + x


Z_GROUPS = [
    [rank(y, zh, core, zl, x) for zh in range(N4) for zl in range(N4)]
    for y in range(N4)
    for core in range(2)
    for x in range(N4)
]
PLANE_GROUPS = [
    [rank(y, zh, core, zl, x) for y in range(N4) for x in range(N4)]
    for zh in range(N4)
    for core in range(2)
    for zl in range(N4)
]
CORE_GROUPS = [[2 * i, 2 * i + 1] for i in range(16)]


def dot(a, b):
    return jnp.dot(a, b, preferred_element_type=F32)


def iota(shape, dim):
    return lax.broadcasted_iota(jnp.int32, shape, dim)


def layer_norm(values):
    mean = jnp.mean(values, axis=-1, keepdims=True)
    centred = values - mean
    var = jnp.mean(centred * centred, axis=-1, keepdims=True)
    return centred * lax.rsqrt(var + 1e-05)


def band_kernel(place, pair, gain, weight, atoms, token, mask, band, pack):
    offset = place[0]
    half = (iota((8, 128), 1) % 32) // 16
    pieces = []
    for k in range(16):
        halves, inside = [], []
        for a in range(2):
            start = offset + 16 * ((k - 1) // 4 + a)
            inside.append((start >= 0) & (start <= 112))
            begin = pl.multiple_of(jnp.clip(start, 0, 112), 16)
            halves.append(pair[4 * k : 4 * k + 4, pl.ds(begin, 16), :])
        block = jnp.concatenate(halves, axis=1).reshape(128, 128).astype(F32)
        normed = (layer_norm(block) * gain[...]).astype(BF16)
        table = lax.dot_general(
            weight[...], normed, (((1,), (1,)), ((), ())), preferred_element_type=F32
        )
        table = jnp.concatenate([table, jnp.zeros_like(table)], axis=0)
        keep = jnp.where(half == 0, inside[0].astype(jnp.int32), inside[1].astype(jnp.int32))
        pieces.append(jnp.where(keep > 0, table, 0.0))
    band[...] = jnp.concatenate(pieces, axis=0).astype(BF16)
    pack[0:64, :] = atoms[...]
    lanes = iota((16, 64), 0)
    local = (token[...] - place[1]).astype(F32)
    live = mask[...].astype(F32)
    rows = jnp.where(lanes == 0, local, jnp.where(lanes == 1, live, 0.0))
    pack[64:80, :] = jnp.concatenate([rows, jnp.zeros_like(rows)], axis=1).astype(BF16)


def logit_kernel(
    place, own, left, right, gain, w_query, w_key, w_value, w_gate,
    logits, state, key_pick, query_pick, value, gate,
):
    ext = jnp.concatenate([left[16:64, :], own[0:64, :], right[0:48, :]], axis=0).astype(F32)
    normed = (layer_norm(ext) * gain[...]).astype(BF16)
    mine = normed[RIM : RIM + ATOMS, :]
    query = dot(mine, w_query[...]).astype(BF16)
    key = dot(normed, w_key[...]).astype(BF16)
    value[...] = dot(normed, w_value[...]).astype(BF16)
    gate[...] = jax.nn.sigmoid(dot(mine, w_gate[...]))
    head_of = iota((ATOMS, 128), 1) // HEAD
    zero = jnp.zeros_like(query)
    wide = jnp.concatenate([jnp.where(head_of == h, query, zero) for h in range(HEADS)], axis=0)
    logits[...] = lax.dot_general(
        wide, key, (((1,), (1,)), ((), ())), preferred_element_type=F32
    ) * (1.0 / HEAD**0.5)
    lane, spot = iota((128, EXT), 0), iota((128, EXT), 1)

    def moved(ref, low, high, shift):
        pick = (lane >= low) & (lane < high) & (lane + shift == spot)
        return dot(ref[64:80, :], pick.astype(F32).astype(BF16))

    facts = (
        moved(left, 16, 64, -16) + moved(own, 0, 64, RIM) + moved(right, 0, 48, RIM + ATOMS)
    )
    where = iota((1, EXT), 1)
    token = facts[0:1, :] + jnp.where(
        where >= RIM + ATOMS, 8.0, jnp.where(where >= RIM, 4.0, 0.0)
    )
    first = (iota((ATOMS, EXT), 0) // QW) * QW
    column = iota((ATOMS, EXT), 1)
    near = (column >= first) & (column < first + KW)
    live = jnp.broadcast_to(facts[1:2, :], (ATOMS, EXT))
    state[...] = jnp.where(near, jnp.where(live > 0.5, 1.0, 0.0), -1.0)
    key_pick[...] = (
        ((lane % 32) == token.astype(jnp.int32) + place[0]).astype(F32).astype(BF16)
    )
    own_row = own[64:80, :].astype(F32)[0:1, :]
    square = iota((ATOMS, 128), 0) == iota((ATOMS, 128), 1)
    own_token = jnp.sum(jnp.where(square, own_row, 0.0), axis=1, keepdims=True)
    query_pick[...] = (iota((ATOMS, 128), 1) // 32 == own_token.astype(jnp.int32)).astype(F32)


def atom_kernel(
    band, logits, state, key_pick, query_pick, value, gate, pack, w_out, mid_gain, w_up, w_down,
    w_single, w_row, w_col, atoms_out, terms,
):
    table = jnp.sum(band[...].astype(F32).reshape(16, 8, 128), axis=0)
    picked = jnp.concatenate([query_pick[...] * table[h : h + 1, :] for h in range(HEADS)], axis=0)
    bias = dot(picked.astype(BF16), key_pick[...])
    states = jnp.concatenate([state[...]] * HEADS, axis=0)
    scores = jnp.where(
        states > 0.5, logits[...] + bias, jnp.where(states > -0.5, -1000000000.0, FAR)
    )
    top = jnp.max(scores, axis=-1, keepdims=True)
    expo = jnp.exp(scores - top)
    weights = (expo / jnp.sum(expo, axis=-1, keepdims=True)).astype(BF16)
    mixed = dot(weights, value[...])
    head_of = iota((ATOMS, 128), 1) // HEAD
    attended = jnp.zeros((ATOMS, 128), F32)
    for h in range(HEADS):
        attended = jnp.where(head_of == h, mixed[h * ATOMS : (h + 1) * ATOMS, :], attended)
    gated = (attended * gate[...]).astype(BF16)
    mid = pack[0:64, :].astype(F32) + dot(gated, w_out[...])
    mid_norm = (layer_norm(mid) * mid_gain[...]).astype(BF16)
    gate_up = dot(mid_norm, w_up[...])
    width = gate_up.shape[1] // 2
    half = 0.5 * gate_up[:, :width]
    hidden = ((half + half * jnp.tanh(half)) * gate_up[:, width:]).astype(BF16)
    out = (mid + dot(hidden, w_down[...])).astype(BF16)
    atoms_out[...] = out
    single = jnp.maximum(dot(out, w_single[...]), 0.0)
    facts = pack[64:80, :].astype(F32)
    chosen = jnp.where(
        (iota((8, 128), 0) % 4).astype(F32) == facts[0:1, :], facts[1:2, :], 0.0
    )[:, 0:64]
    counts = jnp.sum(chosen, axis=-1, keepdims=True)
    chosen = chosen.astype(BF16)
    high = single.astype(BF16)
    low = (single - high.astype(F32)).astype(BF16)
    singles = ((dot(chosen, high) + dot(chosen, low)) / counts).astype(BF16)
    col, row = dot(singles, w_col[...]), dot(singles, w_row[...])
    both = jnp.where(iota((8, 128), 0) < 4, col, row)
    terms[...] = jnp.concatenate([both] * 16, axis=0).astype(BF16)


def spread_kernel(place, came, _after, going):
    tiles = came[...].astype(F32).reshape(16, 8, 128)
    cols, rows = [], jnp.zeros((16, 128), F32)
    for zh in range(N4):
        group = [tiles[zh * N4 + zl] for zl in range(N4)]
        cols.append(jnp.concatenate([t[0:4] for t in group], axis=0))
        mine = jnp.concatenate([t[4:8] for t in group], axis=0)
        rows = jnp.where(place[0] == zh, mine, rows)
    plane = jnp.concatenate([piece for col in cols for piece in (col, rows)], axis=0)
    going[...] = jnp.concatenate([plane] * N4, axis=0).astype(BF16)


def settle_kernel(place, came, _after, cols, rows):
    def ordered(start, low):
        begin = pl.multiple_of(start * 128, 128)
        part = came[pl.ds(begin, 128), :].astype(F32).reshape(N4, 32, 128)
        return jnp.concatenate(
            [
                part[x, low + 4 * zl : low + 4 * zl + 4]
                for zl in range(N4)
                for x in range(N4)
            ],
            axis=0,
        )

    cols[...] = ordered(place[0], 0).astype(BF16)
    rows[...] = ordered(place[1], 16)


def transition_kernel(pair, gain, w_up, w_down, *rest):
    out = rest[-1]
    block = pair[...].reshape(-1, 128).astype(F32)
    normed = (layer_norm(block) * gain[...]).astype(BF16)
    gate_up = dot(normed, w_up[...])
    width = gate_up.shape[1] // 2
    half = 0.5 * gate_up[:, :width]
    hidden = ((half + half * jnp.tanh(half)) * gate_up[:, width:]).astype(BF16)
    total = block + dot(hidden, w_down[...])
    out[...] = total.astype(BF16).reshape(out.shape)


def add_kernel(part, rows, cols, out):
    step = part.shape[0]
    begin = pl.multiple_of(pl.program_id(0) * step, step)
    row = rows[pl.ds(begin, step), :]
    total = part[...].astype(F32) + row[:, None, :] + cols[...].astype(F32)[None, :, :]
    out[...] = total.astype(BF16)


def whole(count):
    return [pl.BlockSpec(memory_space=pltpu.VMEM)] * count


SCALARS = pl.BlockSpec(memory_space=pltpu.SMEM)
PARAMS = pltpu.CompilerParams(vmem_limit_bytes=40 * 1024 * 1024)


def cost(flops, moved, trans=0):
    return pl.CostEstimate(flops=flops, bytes_accessed=moved, transcendentals=trans)


def transition(pair, gain, w_up, w_down, first, last, before=None):
    blocks = (last - first) // PAIR_ROWS
    start = first // PAIR_ROWS
    at = lambda i: (i + start, 0, 0)
    block = pl.BlockSpec((PAIR_ROWS, 128, 128), at)
    fixed = lambda shape: pl.BlockSpec(shape, lambda i: (0, 0))
    specs = [block, fixed((1, 128)), fixed(w_up.shape), fixed(w_down.shape)]
    given = [pair, gain, w_up, w_down]
    if before is not None:
        specs.append(pl.BlockSpec(memory_space=pl.ANY))
        given.append(before)
    count = (last - first) * 128
    return pl.pallas_call(
        transition_kernel,
        grid=(blocks,),
        in_specs=specs,
        out_specs=block,
        out_shape=jax.ShapeDtypeStruct(pair.shape, BF16),
        input_output_aliases={} if before is None else {4: 0},
        compiler_params=PARAMS,
        cost_estimate=cost(count * 4 * 196608, count * 512, count * 512),
    )(*given)


def body(
    pair, atoms, atom_token, atom_mask, bias_gain, w_pair_bias, trans_gain, w_pair_up, w_pair_down,
    atom_gain, w_query, w_key, w_value, w_gate, w_out, mid_gain, w_atom_up, w_atom_down, w_single,
    w_outer_row, w_outer_col,
):
    row, col = lax.axis_index("row"), lax.axis_index("col")
    joint = ("row", "col")
    y, zh, zl = row // 8, (row // 2) % 4, col // 4
    i32 = jnp.int32
    place_band = jnp.stack([64 * row - 128 * col, 4 * (row * 16 + col)]).astype(i32)
    place_shift = (4 * ((col + 3) % 4)).astype(i32)[None]
    place_zh = zh.astype(i32)[None]
    place_end = jnp.stack([zl, y]).astype(i32)
    shape = jax.ShapeDtypeStruct

    band, pack = pl.pallas_call(
        band_kernel,
        in_specs=[SCALARS] + whole(6),
        out_specs=whole(2),
        out_shape=[shape((128, 128), BF16), shape((PACK, 128), BF16)],
        compiler_params=PARAMS,
        cost_estimate=cost(2048 * 2048, 1 << 21),
    )(
        place_band,
        pair,
        bias_gain[None],
        w_pair_bias.T,
        atoms,
        atom_token[None],
        atom_mask[None],
    )
    own_band = lax.all_to_all(band, "col", 0, 0, tiled=True)
    count = 512
    left = lax.ppermute(pack, joint, [(i, i + 1) for i in range(count - 1)])
    right = lax.ppermute(pack, joint, [(i + 1, i) for i in range(count - 1)])
    prepared = pl.pallas_call(
        logit_kernel,
        in_specs=[SCALARS] + whole(8),
        out_specs=whole(6),
        out_shape=[
            shape((HEADS * ATOMS, EXT), F32),
            shape((ATOMS, EXT), F32),
            shape((128, EXT), BF16),
            shape((ATOMS, 128), F32),
            shape((EXT, 128), BF16),
            shape((ATOMS, 128), F32),
        ],
        compiler_params=PARAMS,
        cost_estimate=cost(1 << 24, 1 << 19),
    )(place_shift, pack, left, right, atom_gain[None], w_query, w_key, w_value, w_gate)
    atoms_out, terms = pl.pallas_call(
        atom_kernel,
        in_specs=whole(15),
        out_specs=whole(2),
        out_shape=[shape((ATOMS, 128), BF16), shape((128, 128), BF16)],
        compiler_params=PARAMS,
        cost_estimate=cost(1 << 25, 1 << 20),
    )(
        own_band, *prepared, pack, w_out, mid_gain[None], w_atom_up, w_atom_down, w_single,
        w_outer_row, w_outer_col,
    )
    along = lax.all_to_all(terms, joint, 0, 0, tiled=True, axis_index_groups=Z_GROUPS)
    held, _ = lax.optimization_barrier((trans_gain, terms))
    part = transition(pair, held[None], w_pair_up, w_pair_down, 0, SPLIT)
    hold = pl.BlockSpec(memory_space=pl.ANY)
    going = pl.pallas_call(
        spread_kernel,
        in_specs=[SCALARS] + whole(1) + [hold],
        out_specs=whole(1)[0],
        out_shape=shape((512, 128), BF16),
        compiler_params=PARAMS,
    )(place_zh, along, part)
    came = lax.all_to_all(going, joint, 0, 0, tiled=True, axis_index_groups=PLANE_GROUPS)
    held, _ = lax.optimization_barrier((trans_gain, going))
    part = transition(pair, held[None], w_pair_up, w_pair_down, SPLIT, 64, part)
    cols, rows = pl.pallas_call(
        settle_kernel,
        in_specs=[SCALARS] + whole(1) + [hold],
        out_specs=whole(2),
        out_shape=[shape((64, 128), BF16), shape((64, 128), F32)],
        compiler_params=PARAMS,
    )(place_end, came, part)
    cols = lax.all_gather(cols, "row", axis=0, tiled=True, axis_index_groups=CORE_GROUPS)
    block = pl.BlockSpec((16, 128, 128), lambda i: (i, 0, 0))
    pair_out = pl.pallas_call(
        add_kernel,
        grid=(4,),
        in_specs=[
            block,
            pl.BlockSpec((64, 128), lambda i: (0, 0)),
            pl.BlockSpec((128, 128), lambda i: (0, 0)),
        ],
        out_specs=block,
        out_shape=shape(pair.shape, BF16),
        compiler_params=PARAMS,
    )(part, rows, cols)
    return (atoms_out, pair_out)


def solution(mesh):
    spread = P(("row", "col"))
    in_specs = (P("row", "col", None), P(("row", "col"), None), spread, spread) + (P(),) * 17
    out_specs = (P(("row", "col"), None), P("row", "col", None))
    return jax.shard_map(body, mesh=mesh, in_specs=in_specs, out_specs=out_specs, check_vma=False)
```

time: 284 us -> 77.5 us (0.27)
  the two profiles are of different devices: /device:TPU:2 before, /device:TPU:1 now
where the time goes in v1:
time: 77.5 us; the launch traced here: 77 us
  starting transfers between devices  35.7 us (46%)
  Pallas kernels  20.4 us (26%)
  waiting for transfers between devices  9.66 us (12%)
  local copies, waits for them, and re-layouts  8.2 us (11%)
  blocking collectives  1.83 us (2%)
  between operations  0.97 us (1%)
    pallas_call x2, Pallas kernels, transition(): pl.pallas_call(transition_kernel, grid=(blocks,), in_specs=specs, out_spe...  12.5 us
    all_to_all x1, starting transfers between devices, body(): lax.all_to_all(terms, joint, 0, 0, tiled=True, axis_index_groups=Z_GROUPS)  11.8 us
    all_to_all x1, starting transfers between devices, body(): own_band = lax.all_to_all(band, 'col', 0, 0, tiled=True)  9.01 us
    ppermute x1, starting transfers between devices, body(): right = lax.ppermute(pack, joint, [(i + 1, i) for i in range(count - 1)])  8.67 us
    unnamed x46, local copies, waits for them, and re-layouts  8.2 us
    ppermute x1, waiting for transfers between devices, body(): left = lax.ppermute(pack, joint, [(i, i + 1) for i in range(count - 1)])  6.97 us
    all_to_all x1, starting transfers between devices, body(): lax.all_to_all(going, joint, 0, 0, tiled=True, axis_index_groups=PLANE_GR...  4.3 us
    all_to_all x1, waiting for transfers between devices, body(): lax.all_to_all(terms, joint, 0, 0, tiled=True, axis_index_groups=Z_GROUPS)  2.13 us
  transfers between devices with their start and end apart: 5, of which 3 were waited for; matrix products, arithmetic and copies ran while one was open for 0% of the time, Pallas kernels for 17%

profile of v1, /device:TPU:1, one launch (start us, length us, event | category | flops | bytes accessed | tf_op | source)
XLA Modules:
  0.0 77.0 jit_solution(6450747540285668149)
XLA Ops:
  0.8 1.6 %copy-done = bf16[64,128,128]{2,1,0:T(8,128)(2,1)S(1)} copy-done((bf16[64,128,128]{2,1,0:T(8,128)(2,1)S(1)}, bf16[64,128,128]{2,1,0:T(8,128)(2,1)}, u32[]{:S(2)}) %copy-start) | copy-done | bytes 2097176
  2.4 0.7 copy-done.13
  3.1 0.7 copy-done.14
  3.7 0.7 copy-done.15
  4.4 0.7 copy-done.16
  5.1 0.7 copy-done.17
  5.8 2.1 %shard_map.212 = (bf16[128,128]{1,0:T(8,128)(2,1)}, bf16[80,128]{1,0:T(8,128)(2,1)S(1)}) custom-call(s32[2]{0:T(128)S(1)} %pad_add_fusion.place, bf16[64,128,128]{2,1,0:T(8,128)(2,1)S(1)} %copy-done, f32[1,128]{1,0:T(1,128)S(1)} %bitcast.24, bf16[4,128]{1,0:T(4,128)(2,1)S(1)} %bitcast.23, bf16[64,128]{1,0:T(8,128)(2,1)S(1)} %copy-done.13, ...), custom_call_target="tpu_custom_call" | custom-call | flops 4194304 | bytes 2097152 | tf_op jit(solution)/shard_map/pallas_call | solution.py:275
  7.9 9.0 %all-to-all-start = ((bf16[16,8,128]{2,1,0:T(8,128)(2,1)}), bf16[16,8,128]{2,1,0:T(8,128)(2,1)S(1)}, u32[]{:S(2)}, u32[]{:S(2)}) async-start(bf16[16,8,128]{2,1,0:T(8,128)(2,1)} %bitcast.6), calls=%async_computation | async-start | bytes 65536 | tf_op jit(solution)/shard_map/all_to_all | solution.py:291
  16.9 8.7 %collective-permute-start.1 = (bf16[80,128]{1,0:T(8,128)(2,1)S(1)}, bf16[80,128]{1,0:T(8,128)(2,1)S(1)}, u32[]{:S(2)}, u32[]{:S(2)}) collective-permute-start(bf16[80,128]{1,0:T(8,128)(2,1)S(1)} %get-tuple-element.17.own.pack), channel_id=1, source_target_pairs={{1,0},{2,1},{3,2},{4,3},{5,4},{6,5},{7,6},{8,7},{9,8},{10,9},{11,1... | collective-permute-start | bytes 61448 | tf_op jit(solution)/shard_map/ppermute | solution.py:294
  25.6 1.9 %collective-permute-start = (bf16[80,128]{1,0:T(8,128)(2,1)S(1)}, bf16[80,128]{1,0:T(8,128)(2,1)S(1)}, u32[]{:S(2)}, u32[]{:S(2)}) collective-permute-start(bf16[80,128]{1,0:T(8,128)(2,1)S(1)} %get-tuple-element.17.own.pack), channel_id=1, source_target_pairs={{0,1},{1,2},{2,3},{3,4},{4,5},{5,6},{6,7},{7,8},{8,9},{9,10},{10,1... | collective-permute-start | bytes 61448 | tf_op jit(solution)/shard_map/ppermute | solution.py:293
  27.6 7.0 %collective-permute-done.left = bf16[80,128]{1,0:T(8,128)(2,1)S(1)} collective-permute-done((bf16[80,128]{1,0:T(8,128)(2,1)S(1)}, bf16[80,128]{1,0:T(8,128)(2,1)S(1)}, u32[]{:S(2)}, u32[]{:S(2)}) %collective-permute-start) | collective-permute-done | bytes 20512 | tf_op jit(solution)/shard_map/ppermute | solution.py:293
  35.3 2.1 %shard_map.214 = (bf16[64,128]{1,0:T(8,128)(2,1)}, bf16[128,128]{1,0:T(8,128)(2,1)}) custom-call(bf16[128,128]{1,0:T(8,128)(2,1)S(1)} %bitcast.22, f32[256,160]{1,0:T(8,128)S(1)} %get-tuple-element.18.logits, f32[64,160]{1,0:T(8,128)S(1)} %get-tuple-element.19.state, bf16[128,160]{1,0:T(8,128)(2,1)S(1)} %get-tuple-element.20.key_pick, ...), custom_call_target="tpu_custom_call" | custom-call | flops 33554432 | bytes 1048576 | tf_op jit(solution)/shard_map/pallas_call | solution.py:310
  37.3 11.8 %all-to-all-start.1 = ((bf16[16,8,128]{2,1,0:T(8,128)(2,1)}), bf16[16,8,128]{2,1,0:T(8,128)(2,1)S(1)}, u32[]{:S(2)}, u32[]{:S(2)}) async-start(bf16[16,8,128]{2,1,0:T(8,128)(2,1)} %bitcast.12), calls=%async_computation.1 | async-start | bytes 65536 | tf_op jit(solution)/shard_map/all_to_all | solution.py:321
  49.2 1.6 %copy-done.1 = bf16[64,128,128]{2,1,0:T(8,128)(2,1)S(1)} copy-done((bf16[64,128,128]{2,1,0:T(8,128)(2,1)S(1)}, bf16[64,128,128]{2,1,0:T(8,128)(2,1)}, u32[]{:S(2)}) %copy-start.1) | copy-done | bytes 2097176
  50.8 7.8 %shard_map.215._after.rest_0_ = bf16[64,128,128]{2,1,0:T(8,128)(2,1)S(1)} custom-call(bf16[64,128,128]{2,1,0:T(8,128)(2,1)S(1)} %copy-done.1, f32[1,128]{1,0:T(1,128)S(1)} %bitcast.29, bf16[128,1024]{1,0:T(8,128)(2,1)S(1)} %copy-done.20, bf16[512,128]{1,0:T(8,128)(2,1)S(1)} %copy-done.21), custom_call_target="tpu_custom_call" | custom-call | flops 4026531840 | bytes 2621440 | tf_op jit(solution)/shard_map/pallas_call | solution.py:248
  58.6 2.1 %all-to-all-done.1 = bf16[16,8,128]{2,1,0:T(8,128)(2,1)S(1)} async-done(((bf16[16,8,128]{2,1,0:T(8,128)(2,1)}), bf16[16,8,128]{2,1,0:T(8,128)(2,1)S(1)}, u32[]{:S(2)}, u32[]{:S(2)}) %all-to-all-start.1) | async-done | bytes 32800 | tf_op jit(solution)/shard_map/all_to_all | solution.py:321
  60.7 0.7 shard_map.216
  61.4 4.3 %all-to-all-start.2 = ((bf16[16,32,128]{2,1,0:T(8,128)(2,1)}), bf16[16,32,128]{2,1,0:T(8,128)(2,1)S(1)}, u32[]{:S(2)}, u32[]{:S(2)}) async-start(bf16[16,32,128]{2,1,0:T(8,128)(2,1)} %bitcast.18), calls=%async_computation.2 | async-start | bytes 262144 | tf_op jit(solution)/shard_map/all_to_all | solution.py:332
  65.7 1.6 %copy-done.2 = bf16[64,128,128]{2,1,0:T(8,128)(2,1)S(1)} copy-done((bf16[64,128,128]{2,1,0:T(8,128)(2,1)S(1)}, bf16[64,128,128]{2,1,0:T(8,128)(2,1)}, u32[]{:S(2)}) %copy-start.2) | copy-done | bytes 2097176
  67.3 4.7 %shard_map.217._after.part = bf16[64,128,128]{2,1,0:T(8,128)(2,1)S(1)} custom-call(bf16[64,128,128]{2,1,0:T(8,128)(2,1)S(1)} %copy-done.2, f32[1,128]{1,0:T(1,128)S(1)} %bitcast.30, bf16[128,1024]{1,0:T(8,128)(2,1)S(1)} %copy-done.20, bf16[512,128]{1,0:T(8,128)(2,1)S(1)} %copy-done.21, ...), custom_call_target="tpu_custom_call", output_to_operand_aliasing={{}: (4, {})} | custom-call | flops 2415919104 | bytes 1572864 | tf_op jit(solution)/shard_map/pallas_call | solution.py:248
  72.0 0.6 all-to-all-done.2
  72.6 0.6 shard_map.218
  73.1 1.8 %all_gather.3.cols = bf16[128,128]{1,0:T(8,128)(2,1)S(1)} all-gather(bf16[64,128]{1,0:T(8,128)(2,1)S(1)} %get-tuple-element.29), channel_id=1, replica_groups={{0,16},{32,48},{64,80},{96,112},{128,144},{160,176},{192,208},{224,240}..., dimensions={0}, use_global_device_ids=true | all-gather | bytes 49152 | tf_op jit(solution)/shard_map/all_gather | solution.py:342
  75.0 2.0 %shard_map.219 = bf16[64,128,128]{2,1,0:T(8,128)(2,1)} custom-call(bf16[64,128,128]{2,1,0:T(8,128)(2,1)S(1)} %shard_map.217._after.part, f32[64,128]{1,0:T(8,128)S(1)} %get-tuple-element.28.rows, bf16[128,128]{1,0:T(8,128)(2,1)S(1)} %all_gather.3.cols), custom_call_target="tpu_custom_call" | custom-call | tf_op jit(solution)/shard_map/pallas_call | solution.py:344
  (43 shorter events, 0.8 us)
Async XLA Ops:
  0.6 34.0 %copy-start.18 = (f32[128]{0:T(128)S(1)}, f32[128]{0:T(128)}, u32[]{:S(2)}) copy-start(f32[128]{0:T(128)} %param.30) | copy-start | bytes 1540
  0.6 34.5 %copy-start.19 = (f32[128]{0:T(128)S(1)}, f32[128]{0:T(128)}, u32[]{:S(2)}) copy-start(f32[128]{0:T(128)} %param.36) | copy-start | bytes 1540
  0.7 34.5 %copy-start.8 = (bf16[128,128]{1,0:T(8,128)(2,1)S(1)}, bf16[128,128]{1,0:T(8,128)(2,1)}, u32[]{:S(2)}) copy-start(bf16[128,128]{1,0:T(8,128)(2,1)} %w_out.1) | copy-start | bytes 98308
  0.7 48.5 %copy-start.22 = (f32[128]{0:T(128)S(1)}, f32[128]{0:T(128)}, u32[]{:S(2)}) copy-start(f32[128]{0:T(128)} %param.27) | copy-start | bytes 1540
  0.8 1.6 %copy-start = (bf16[64,128,128]{2,1,0:T(8,128)(2,1)S(1)}, bf16[64,128,128]{2,1,0:T(8,128)(2,1)}, u32[]{:S(2)}) copy-start(bf16[64,128,128]{2,1,0:T(8,128)(2,1)} %pair.5) | copy-start | bytes 6291460
  2.3 0.7 copy-start.13
  5.7 28.9 %copy-start.9 = (bf16[128,128]{1,0:T(8,128)(2,1)S(1)}, bf16[128,128]{1,0:T(8,128)(2,1)}, u32[]{:S(2)}) copy-start(bf16[128,128]{1,0:T(8,128)(2,1)} %w_query.1) | copy-start | bytes 98308
  5.7 28.9 %copy-start.10 = (bf16[128,128]{1,0:T(8,128)(2,1)S(1)}, bf16[128,128]{1,0:T(8,128)(2,1)}, u32[]{:S(2)}) copy-start(bf16[128,128]{1,0:T(8,128)(2,1)} %w_key.1) | copy-start | bytes 98308
  5.7 28.9 %copy-start.11 = (bf16[128,128]{1,0:T(8,128)(2,1)S(1)}, bf16[128,128]{1,0:T(8,128)(2,1)}, u32[]{:S(2)}) copy-start(bf16[128,128]{1,0:T(8,128)(2,1)} %w_value.1) | copy-start | bytes 98308
  5.7 28.9 %copy-start.12 = (bf16[128,128]{1,0:T(8,128)(2,1)S(1)}, bf16[128,128]{1,0:T(8,128)(2,1)}, u32[]{:S(2)}) copy-start(bf16[128,128]{1,0:T(8,128)(2,1)} %w_gate.1) | copy-start | bytes 98308
  5.7 29.5 %copy-start.3 = (bf16[128,512]{1,0:T(8,128)(2,1)S(1)}, bf16[128,512]{1,0:T(8,128)(2,1)}, u32[]{:S(2)}) copy-start(bf16[128,512]{1,0:T(8,128)(2,1)} %w_up.3) | copy-start | bytes 393220
  5.7 29.5 %copy-start.4 = (bf16[128,384]{1,0:T(8,128)(2,1)S(1)}, bf16[128,384]{1,0:T(8,128)(2,1)}, u32[]{:S(2)}) copy-start(bf16[128,384]{1,0:T(8,128)(2,1)} %w_single.1) | copy-start | bytes 294916
  5.7 29.5 %copy-start.5 = (bf16[384,128]{1,0:T(8,128)(2,1)S(1)}, bf16[384,128]{1,0:T(8,128)(2,1)}, u32[]{:S(2)}) copy-start(bf16[384,128]{1,0:T(8,128)(2,1)} %w_row.1) | copy-start | bytes 294916
  5.8 29.5 %copy-start.6 = (bf16[384,128]{1,0:T(8,128)(2,1)S(1)}, bf16[384,128]{1,0:T(8,128)(2,1)}, u32[]{:S(2)}) copy-start(bf16[384,128]{1,0:T(8,128)(2,1)} %w_col.1) | copy-start | bytes 294916
  5.8 29.5 %copy-start.7 = (bf16[256,128]{1,0:T(8,128)(2,1)S(1)}, bf16[256,128]{1,0:T(8,128)(2,1)}, u32[]{:S(2)}) copy-start(bf16[256,128]{1,0:T(8,128)(2,1)} %w_down.3) | copy-start | bytes 196612
  5.8 43.4 %copy-start.20 = (bf16[128,1024]{1,0:T(8,128)(2,1)S(1)}, bf16[128,1024]{1,0:T(8,128)(2,1)}, u32[]{:S(2)}) copy-start(bf16[128,1024]{1,0:T(8,128)(2,1)} %w_up.5) | copy-start | bytes 786436
  5.8 43.4 %copy-start.21 = (bf16[512,128]{1,0:T(8,128)(2,1)S(1)}, bf16[512,128]{1,0:T(8,128)(2,1)}, u32[]{:S(2)}) copy-start(bf16[512,128]{1,0:T(8,128)(2,1)} %w_down.5) | copy-start | bytes 393220
  7.9 27.3 %all-to-all-start = ((bf16[16,8,128]{2,1,0:T(8,128)(2,1)}), bf16[16,8,128]{2,1,0:T(8,128)(2,1)S(1)}, u32[]{:S(2)}, u32[]{:S(2)}) async-start(bf16[16,8,128]{2,1,0:T(8,128)(2,1)} %bitcast.6), calls=%async_computation | async-start | bytes 65536 | tf_op jit(solution)/shard_map/all_to_all | solution.py:291
  16.9 10.7 %collective-permute-start.1 = (bf16[80,128]{1,0:T(8,128)(2,1)S(1)}, bf16[80,128]{1,0:T(8,128)(2,1)S(1)}, u32[]{:S(2)}, u32[]{:S(2)}) collective-permute-start(bf16[80,128]{1,0:T(8,128)(2,1)S(1)} %get-tuple-element.17.own.pack), channel_id=1, source_target_pairs={{1,0},{2,1},{3,2},{4,3},{5,4},{6,5},{7,6},{8,7},{9,8},{10,9},{11,1... | collective-permute-start | bytes 61448 | tf_op jit(solution)/shard_map/ppermute | solution.py:294
  25.6 9.0 %collective-permute-start = (bf16[80,128]{1,0:T(8,128)(2,1)S(1)}, bf16[80,128]{1,0:T(8,128)(2,1)S(1)}, u32[]{:S(2)}, u32[]{:S(2)}) collective-permute-start(bf16[80,128]{1,0:T(8,128)(2,1)S(1)} %get-tuple-element.17.own.pack), channel_id=1, source_target_pairs={{0,1},{1,2},{2,3},{3,4},{4,5},{5,6},{6,7},{7,8},{8,9},{9,10},{10,1... | collective-permute-start | bytes 61448 | tf_op jit(solution)/shard_map/ppermute | solution.py:293
  37.3 23.4 %all-to-all-start.1 = ((bf16[16,8,128]{2,1,0:T(8,128)(2,1)}), bf16[16,8,128]{2,1,0:T(8,128)(2,1)S(1)}, u32[]{:S(2)}, u32[]{:S(2)}) async-start(bf16[16,8,128]{2,1,0:T(8,128)(2,1)} %bitcast.12), calls=%async_computation.1 | async-start | bytes 65536 | tf_op jit(solution)/shard_map/all_to_all | solution.py:321
  49.2 1.6 %copy-start.1 = (bf16[64,128,128]{2,1,0:T(8,128)(2,1)S(1)}, bf16[64,128,128]{2,1,0:T(8,128)(2,1)}, u32[]{:S(2)}) copy-start(bf16[64,128,128]{2,1,0:T(8,128)(2,1)} %pair.5) | copy-start | bytes 6291460
  61.4 11.1 %all-to-all-start.2 = ((bf16[16,32,128]{2,1,0:T(8,128)(2,1)}), bf16[16,32,128]{2,1,0:T(8,128)(2,1)S(1)}, u32[]{:S(2)}, u32[]{:S(2)}) async-start(bf16[16,32,128]{2,1,0:T(8,128)(2,1)} %bitcast.18), calls=%async_computation.2 | async-start | bytes 262144 | tf_op jit(solution)/shard_map/all_to_all | solution.py:332
  65.7 1.6 %copy-start.2 = (bf16[64,128,128]{2,1,0:T(8,128)(2,1)S(1)}, bf16[64,128,128]{2,1,0:T(8,128)(2,1)}, u32[]{:S(2)}) copy-start(bf16[64,128,128]{2,1,0:T(8,128)(2,1)} %pair.5) | copy-start | bytes 6291460
  (4 other events, 2.6 us)

commit v2 on v1

v2 whole, which is shorter than its diff:
```python
import functools

import jax
import jax.numpy as jnp
from jax import lax
from jax.experimental import pallas as pl
from jax.experimental.pallas import tpu as pltpu
from jax.sharding import PartitionSpec as P

F32 = jnp.float32
BF16 = jnp.bfloat16
N4 = 4
QW = 32
KW = 128
RIM = (KW - QW) // 2
ATOMS = 64
EXT = ATOMS + 2 * RIM
HEADS = 4
HEAD = 32
PACK = 80
FAR = -3.0e38
PHASES = (0, 2, 5, 8)
PAIR_ROWS = 8
STEPS = 2


def rank(y, zh, core, zl, x):
    return ((y * N4 + zh) * 2 + core) * 16 + zl * N4 + x


Z_ORDER = ((2, 0),) + tuple(
    (zh, zl) for zh in (0, 1, 3, 2) for zl in range(N4) if (zh, zl) != (2, 0)
)
PLANE_ORDER = (3, 0, 1, 2)
Z_GROUPS = [
    [rank(y, zh, core, zl, x) for zh, zl in Z_ORDER]
    for y in range(N4)
    for core in range(2)
    for x in range(N4)
]
PLANE_GROUPS = [
    [rank(y, zh, core, zl, x) for y in PLANE_ORDER for x in PLANE_ORDER]
    for zh in range(N4)
    for core in range(2)
    for zl in range(N4)
]


def leader(row):
    return jnp.where(row < 16, 4, 8) + lax.rem(row // 2, 4)


ROW_GROUPS = [
    [16 * row + (4 * (1 if row < 16 else 2) + (row // 2) % 4 + j) % 16 for j in range(16)]
    for row in range(32)
]
CORE_GROUPS = [[2 * i, 2 * i + 1] for i in range(16)]


def dot(a, b):
    return jnp.dot(a, b, preferred_element_type=F32)


def iota(shape, dim):
    return lax.broadcasted_iota(jnp.int32, shape, dim)


def layer_norm(values):
    mean = jnp.mean(values, axis=-1, keepdims=True)
    centred = values - mean
    var = jnp.mean(centred * centred, axis=-1, keepdims=True)
    return centred * lax.rsqrt(var + 1e-05)


def band_kernel(
    pair, gain, weight, atoms, token, mask, band, pack,
    tile, gain_v, weight_v, atoms_v, token_v, mask_v, tile_sem, small_sem,
):
    row, col = lax.axis_index("row"), lax.axis_index("col")
    offset = 64 * row - 128 * col
    base = pl.multiple_of(jnp.where(offset >= 64, 48, 0), 16)
    close = (offset >= -64) & (offset <= 128)
    each = pair.shape[0] // STEPS
    big = [
        pltpu.make_async_copy(
            pair.at[pl.ds(each * g, each), pl.ds(base, 80)],
            tile.at[pl.ds(each * g, each)],
            tile_sem.at[g],
        )
        for g in range(STEPS)
    ]

    @pl.when(close)
    def _():
        for copy in big:
            copy.start()

    small = [
        pltpu.make_async_copy(src, dst, small_sem.at[i])
        for i, (src, dst) in enumerate(
            [(gain, gain_v), (weight, weight_v), (atoms, atoms_v), (token, token_v), (mask, mask_v)]
        )
    ]
    for copy in small:
        copy.start()
    band[...] = jnp.zeros_like(band)
    for copy in small:
        copy.wait()
    pack[0:64, :] = atoms_v[...]
    lanes = iota((8, 64), 0)
    local = (token_v[...] - 4 * (row * 16 + col)).astype(F32)
    live = mask_v[...].astype(F32)
    facts = jnp.where(lanes == 0, local, jnp.where(lanes == 1, live, 0.0))
    facts = jnp.concatenate([facts, jnp.zeros_like(facts)], axis=1)
    none = jnp.zeros_like(facts)
    pack[64:80, :] = jnp.concatenate([facts, none], axis=0).astype(BF16)
    first = leader(row)

    def slot(k, low, count):
        return pl.ds(pl.multiple_of(64 * lax.rem(k + 16 - first, 16) + low, 16), count)

    @pl.when(col < 15)
    def _():
        band[slot(col + 1, 0, 48), :] = atoms_v[16:64, :]

    @pl.when(col > 0)
    def _():
        band[slot(col - 1, 0, 48), :] = atoms_v[0:48, :]

    @pl.when(jnp.logical_not(close))
    def _():
        last = jnp.concatenate([none, facts], axis=0).astype(BF16)
        for k in range(16):
            band[64 * k + 48 : 64 * k + 64, :] = last

    @pl.when(close)
    def _():
        half = (iota((8, 128), 1) % 32) // 16
        for g in range(STEPS):
            each = 16 // STEPS
            big[g].wait()
            pieces, inside = [], []
            for k in range(each * g, each * g + each):
                halves = []
                for a in range(2):
                    start = offset + 16 * ((k - 1) // 4 + a)
                    inside.append(((start >= 0) & (start <= 112)).astype(jnp.int32))
                    begin = pl.multiple_of(jnp.clip(start - base, 0, 64), 16)
                    halves.append(tile[4 * k : 4 * k + 4, pl.ds(begin, 16), :])
                pieces.append(jnp.concatenate(halves, axis=1).reshape(128, 128))
            block = jnp.concatenate(pieces, axis=0)
            normed = (layer_norm(block.astype(F32)) * gain_v[...]).astype(BF16)
            table = lax.dot_general(
                weight_v[...], normed, (((1,), (1,)), ((), ())), preferred_element_type=F32
            )
            table = jnp.concatenate([table, jnp.zeros_like(table)], axis=0)
            for j in range(each):
                keep = jnp.where(half == 0, inside[2 * j], inside[2 * j + 1])
                mine = jnp.where(keep > 0, table[:, 128 * j : 128 * j + 128], 0.0)
                last = jnp.concatenate([mine, facts], axis=0).astype(BF16)
                band[slot(each * g + j, 48, 16), :] = last


def atom_kernel(
    band, cross, pack, gain, w_query, w_key, w_value, w_gate, w_out, mid_gain, w_up, w_down,
    w_single, w_row, w_col, _after, atoms_out, terms,
):
    row, col = lax.axis_index("row"), lax.axis_index("col")
    own = pack[...].astype(F32)
    far = cross[...].astype(F32)

    first = leader(row)

    def side(other, low):
        inside = (other >= 0) & (other < 16)
        start = 64 * lax.rem(jnp.clip(other, 0, 15) + 16 - first, 16)
        tile = band[pl.ds(pl.multiple_of(start, 64), 64), :].astype(F32)
        atoms = jnp.where(inside, tile[0:48, :], far[low : low + 48, :])
        return atoms, jnp.where(inside, tile[56:64, :], far[64:72, :])

    left, left_facts = side(col - 1, 16)
    right, right_facts = side(col + 1, 0)
    own_facts = own[64:72, :]
    ext = jnp.concatenate([left, own[0:64, :], right], axis=0)
    normed = (layer_norm(ext) * gain[...]).astype(BF16)
    mine = normed[RIM : RIM + ATOMS, :]
    query = dot(mine, w_query[...]).astype(BF16)
    key = dot(normed, w_key[...]).astype(BF16)
    value = dot(normed, w_value[...]).astype(BF16)
    gate = jax.nn.sigmoid(dot(mine, w_gate[...]))
    head_of = iota((ATOMS, 128), 1) // HEAD
    zero = jnp.zeros_like(query)
    wide = jnp.concatenate([jnp.where(head_of == h, query, zero) for h in range(HEADS)], axis=0)
    logits = lax.dot_general(
        wide, key, (((1,), (1,)), ((), ())), preferred_element_type=F32
    ) * (1.0 / HEAD**0.5)
    lane, spot = iota((128, EXT), 0), iota((128, EXT), 1)

    def moved(facts, low, high, shift):
        pick = (lane >= low) & (lane < high) & (lane + shift == spot)
        return dot(facts.astype(BF16), pick.astype(F32).astype(BF16))

    facts = (
        moved(left_facts, 16, 64, -16)
        + moved(own_facts, 0, 64, RIM)
        + moved(right_facts, 0, 48, RIM + ATOMS)
    )
    where = iota((1, EXT), 1)
    token = facts[0:1, :] + jnp.where(
        where >= RIM + ATOMS, 8.0, jnp.where(where >= RIM, 4.0, 0.0)
    )
    first = (iota((ATOMS, EXT), 0) // QW) * QW
    column = iota((ATOMS, EXT), 1)
    near = (column >= first) & (column < first + KW)
    live = jnp.broadcast_to(facts[1:2, :], (ATOMS, EXT))
    state = jnp.where(near, jnp.where(live > 0.5, 1.0, 0.0), -1.0)
    shift = 4 * lax.rem(col + 3, 4)
    key_pick = ((lane % 32) == token.astype(jnp.int32) + shift).astype(F32).astype(BF16)
    square = iota((ATOMS, 128), 0) == iota((ATOMS, 128), 1)
    own_token = jnp.sum(jnp.where(square, own_facts[0:1, :], 0.0), axis=1, keepdims=True)
    query_pick = (iota((ATOMS, 128), 1) // 32 == own_token.astype(jnp.int32)).astype(F32)

    table = jnp.zeros((16, 128), F32)
    for k in range(16):
        table = table + band[64 * k + 48 : 64 * k + 64, :].astype(F32)
    picked = jnp.concatenate([query_pick * table[h : h + 1, :] for h in range(HEADS)], axis=0)
    bias = dot(picked.astype(BF16), key_pick)
    states = jnp.concatenate([state] * HEADS, axis=0)
    scores = jnp.where(states > 0.5, logits + bias, jnp.where(states > -0.5, -1000000000.0, FAR))
    top = jnp.max(scores, axis=-1, keepdims=True)
    expo = jnp.exp(scores - top)
    weights = (expo / jnp.sum(expo, axis=-1, keepdims=True)).astype(BF16)
    mixed = dot(weights, value)
    attended = jnp.zeros((ATOMS, 128), F32)
    for h in range(HEADS):
        attended = jnp.where(head_of == h, mixed[h * ATOMS : (h + 1) * ATOMS, :], attended)
    gated = (attended * gate).astype(BF16)
    mid = own[0:64, :] + dot(gated, w_out[...])
    mid_norm = (layer_norm(mid) * mid_gain[...]).astype(BF16)
    gate_up = dot(mid_norm, w_up[...])
    width = gate_up.shape[1] // 2
    half = 0.5 * gate_up[:, :width]
    hidden = ((half + half * jnp.tanh(half)) * gate_up[:, width:]).astype(BF16)
    out = (mid + dot(hidden, w_down[...])).astype(BF16)
    atoms_out[...] = out
    single = jnp.maximum(dot(out, w_single[...]), 0.0)
    chosen = jnp.where(
        (iota((8, 128), 0) % 4).astype(F32) == own_facts[0:1, :], own_facts[1:2, :], 0.0
    )[:, 0:64]
    counts = jnp.sum(chosen, axis=-1, keepdims=True)
    chosen = chosen.astype(BF16)
    high = single.astype(BF16)
    low = (single - high.astype(F32)).astype(BF16)
    singles = ((dot(chosen, high) + dot(chosen, low)) / counts).astype(BF16)
    col_terms, row_terms = dot(singles, w_col[...]), dot(singles, w_row[...])
    both = jnp.where(iota((8, 128), 0) < 4, col_terms, row_terms)
    terms[...] = jnp.concatenate([both] * 16, axis=0).astype(BF16)


def spread_kernel(came, _after, going):
    own_zh = lax.rem(lax.axis_index("row") // 2, 4)
    tiles = came[...].astype(F32).reshape(16, 8, 128)
    cols, rows = [], jnp.zeros((16, 128), F32)
    for zh in range(N4):
        group = [tiles[Z_ORDER.index((zh, zl))] for zl in range(N4)]
        cols.append(jnp.concatenate([t[0:4] for t in group], axis=0))
        mine = jnp.concatenate([t[4:8] for t in group], axis=0)
        rows = jnp.where(own_zh == zh, mine, rows)
    plane = jnp.concatenate([piece for x in PLANE_ORDER for piece in (cols[x], rows)], axis=0)
    going[...] = jnp.concatenate([plane] * N4, axis=0).astype(BF16)


def transition_kernel(given, gain, w_up, w_down, _after, out, normed, sem, *, phase):
    low, high = PHASES[phase], PHASES[phase + 1]

    def rows(i):
        return pl.ds(pl.multiple_of(i * PAIR_ROWS, PAIR_ROWS), PAIR_ROWS)

    def norm(i):
        values = out[rows(i)].reshape(-1, 128).astype(F32)
        return (layer_norm(values) * gain[...]).astype(BF16)

    def fetch(i):
        return pltpu.make_async_copy(given.at[rows(i)], out.at[rows(i)], sem.at[i])

    count = PHASES[-1] if phase == 0 else 0
    for i in range(count):
        fetch(i).start()
    for i in range(min(count, 2)):
        fetch(i).wait()
    normed[low % 2] = norm(low)

    @pl.loop(low, high)
    def _(i):
        current = normed[lax.rem(i, 2)]
        following = norm(jnp.minimum(i + 1, high - 1))
        gate_up = dot(current, w_up[...])
        width = gate_up.shape[1] // 2
        half = (0.5 * gate_up[:, :width]).astype(BF16)
        hidden = (half + half * jnp.tanh(half)) * gate_up[:, width:].astype(BF16)
        total = out[rows(i)].reshape(-1, 128).astype(F32) + dot(hidden, w_down[...])
        normed[lax.rem(i + 1, 2)] = following
        out[rows(i)] = total.astype(BF16).reshape(PAIR_ROWS, 128, 128)
        if count:

            @pl.when(i + 2 < count)
            def _():
                fetch(i + 2).wait()

    for i in range(high + 2, count):
        fetch(i).wait()


def add_kernel(part, came, out, done, sem):
    row, col = lax.axis_index("row"), lax.axis_index("col")
    core = lax.rem(row, 2)

    def ordered(start, low):
        piece = came[pl.ds(pl.multiple_of(start, 128), 128), :].astype(F32).reshape(N4, 32, 128)
        return jnp.concatenate(
            [
                piece[PLANE_ORDER.index(x), low + 4 * zl : low + 4 * zl + 4]
                for zl in range(N4)
                for x in range(N4)
            ],
            axis=0,
        )

    zl, y = col // 4, row // 8
    cols = jnp.concatenate(
        [ordered(512 * b + 128 * lax.rem(zl + 1, 4), 0) for b in range(2)], axis=0
    )
    rows = ordered(512 * core + 128 * lax.rem(y + 1, 4), 16)
    copies = []
    for at in range(0, part.shape[0], PAIR_ROWS):
        span = pl.ds(at, PAIR_ROWS)
        total = part[span].astype(F32) + rows[at : at + PAIR_ROWS][:, None, :] + cols[None, :, :]
        done[span] = total.astype(BF16)
        copies.append(pltpu.make_async_copy(done.at[span], out.at[span], sem.at[at // PAIR_ROWS]))
        copies[-1].start()
    for copy in copies:
        copy.wait()


def whole(count):
    return [pl.BlockSpec(memory_space=pltpu.VMEM)] * count


HBM = pl.BlockSpec(memory_space=pltpu.HBM)
ANY = pl.BlockSpec(memory_space=pl.ANY)
SCALARS = pl.BlockSpec(memory_space=pltpu.SMEM)
PARAMS = pltpu.CompilerParams(vmem_limit_bytes=40 * 1024 * 1024)


def cost(flops, moved, trans=0):
    return pl.CostEstimate(flops=flops, bytes_accessed=moved, transcendentals=trans)


def in_hbm(array):
    return pltpu.with_memory_space_constraint(array, pltpu.HBM)


def transition(held, gain, w_up, w_down, phase, after):
    count = 128 * PAIR_ROWS * (PHASES[phase + 1] - PHASES[phase])
    given = HBM if phase == 0 else whole(1)[0]
    return pl.pallas_call(
        functools.partial(transition_kernel, phase=phase),
        in_specs=[given] + whole(3) + [ANY],
        out_specs=whole(1)[0],
        out_shape=jax.ShapeDtypeStruct(held.shape, BF16),
        input_output_aliases={0: 0} if phase else {},
        scratch_shapes=[
            pltpu.VMEM((2, 128 * PAIR_ROWS, 128), BF16),
            pltpu.SemaphoreType.DMA((PHASES[-1],)),
        ],
        compiler_params=PARAMS,
        cost_estimate=cost(count * 4 * 196608, count * 512, count * 512),
    )(held if phase else in_hbm(held), gain, w_up, w_down, after)


def near_diagonal(pair, bias_gain, w_pair_bias, atoms, atom_token, atom_mask):
    return pl.pallas_call(
        band_kernel,
        in_specs=[HBM] * 6,
        out_specs=whole(2),
        out_shape=[
            jax.ShapeDtypeStruct((1024, 128), BF16),
            jax.ShapeDtypeStruct((PACK, 128), BF16),
        ],
        scratch_shapes=[
            pltpu.VMEM((64, 80, 128), BF16),
            pltpu.VMEM((1, 128), F32),
            pltpu.VMEM((4, 128), BF16),
            pltpu.VMEM((64, 128), BF16),
            pltpu.VMEM((1, 64), jnp.int32),
            pltpu.VMEM((1, 64), jnp.int32),
            pltpu.SemaphoreType.DMA((STEPS,)),
            pltpu.SemaphoreType.DMA((5,)),
        ],
        compiler_params=PARAMS,
        cost_estimate=cost(2048 * 2048, 1 << 21),
    )(
        in_hbm(pair),
        in_hbm(bias_gain[None]),
        in_hbm(w_pair_bias.T),
        in_hbm(atoms),
        in_hbm(atom_token[None]),
        in_hbm(atom_mask[None]),
    )


def atom_block(band, cross, pack, gain, w_qkvg, w_out, mid_gain, w_rest, after):
    return pl.pallas_call(
        atom_kernel,
        in_specs=whole(15) + [ANY],
        out_specs=whole(2),
        out_shape=[
            jax.ShapeDtypeStruct((ATOMS, 128), BF16),
            jax.ShapeDtypeStruct((128, 128), BF16),
        ],
        compiler_params=PARAMS,
        cost_estimate=cost(1 << 25, 1 << 20),
    )(band, cross, pack, gain[None], *w_qkvg, w_out, mid_gain[None], *w_rest, after)


def spread_terms(along, after):
    return pl.pallas_call(
        spread_kernel,
        in_specs=whole(1) + [ANY],
        out_specs=whole(1)[0],
        out_shape=jax.ShapeDtypeStruct((512, 128), BF16),
        compiler_params=PARAMS,
    )(along, after)


def add_terms(held, came):
    return pl.pallas_call(
        add_kernel,
        in_specs=whole(2),
        out_specs=HBM,
        out_shape=jax.ShapeDtypeStruct(held.shape, BF16),
        scratch_shapes=[
            pltpu.VMEM(held.shape, BF16),
            pltpu.SemaphoreType.DMA((held.shape[0] // PAIR_ROWS,)),
        ],
        compiler_params=PARAMS,
    )(held, came)


def body(
    pair, atoms, atom_token, atom_mask, bias_gain, w_pair_bias, trans_gain, w_pair_up, w_pair_down,
    atom_gain, w_query, w_key, w_value, w_gate, w_out, mid_gain, w_atom_up, w_atom_down, w_single,
    w_outer_row, w_outer_col,
):
    joint = ("row", "col")
    band, pack = near_diagonal(pair, bias_gain, w_pair_bias, atoms, atom_token, atom_mask)
    band = lax.all_to_all(band, joint, 0, 0, tiled=True, axis_index_groups=ROW_GROUPS)
    ends = [(16 * i + 15, 16 * i + 16) for i in range(31)]
    cross = lax.ppermute(pack, joint, ends + [(j, i) for i, j in ends])
    trans = (trans_gain[None], w_pair_up, w_pair_down)
    held = transition(pair, *trans, 0, pack)
    w_qkvg = (w_query, w_key, w_value, w_gate)
    w_rest = (w_atom_up, w_atom_down, w_single, w_outer_row, w_outer_col)
    atoms_out, terms = atom_block(
        band, cross, pack, atom_gain, w_qkvg, w_out, mid_gain, w_rest, held
    )
    along = lax.all_to_all(terms, joint, 0, 0, tiled=True, axis_index_groups=Z_GROUPS)
    held = transition(held, *trans, 1, terms)
    going = spread_terms(along, held)
    came = lax.all_to_all(going, joint, 0, 0, tiled=True, axis_index_groups=PLANE_GROUPS)
    held = transition(held, *trans, 2, going)
    came, held = lax.optimization_barrier((came, held))
    came = lax.all_gather(came, "row", axis=0, tiled=True, axis_index_groups=CORE_GROUPS)
    return (atoms_out, add_terms(held, came))


def solution(mesh):
    spread = P(("row", "col"))
    in_specs = (P("row", "col", None), P(("row", "col"), None), spread, spread) + (P(),) * 17
    out_specs = (P(("row", "col"), None), P("row", "col", None))
    return jax.shard_map(body, mesh=mesh, in_specs=in_specs, out_specs=out_specs, check_vma=False)
```

time: 77.5 us -> 60.8 us (0.78)
  waiting for transfers between devices: 9.66 us -> 0.01 us
  local copies, waits for them, and re-layouts: 8.2 us -> 0.09 us
  blocking collectives: 1.83 us -> 4.72 us
  Pallas kernels: 20.4 us -> 18.1 us
    unnamed x46 -> x30, local copies, waits for them, and re-layouts: 8.2 us -> 0.09 us
    ppermute x2 -> x1, waiting for transfers between devices: 6.97 us -> 0.01 us  [body(): cross = lax.ppermute(pack, joint, ends + [(j, i) for i, j in ends])]
    all_to_all x1, starting transfers between devices: 4.3 us -> 7.82 us  [body(): lax.all_to_all(going, joint, 0, 0, tiled=True, axis_index_groups=PLANE_GR...]
    all_gather x1, blocking collectives: 1.83 us -> 4.72 us  [body(): lax.all_gather(came, 'row', axis=0, tiled=True, axis_index_groups=CORE_GR...]
    ppermute x2 -> x1, starting transfers between devices: 10.6 us -> 8.3 us  [body(): cross = lax.ppermute(pack, joint, ends + [(j, i) for i, j in ends])]
    pallas_call x8 -> x7, Pallas kernels: 20.4 us -> 18.1 us  [the longest x3 10.6 us: transition(): pl.pallas_call(functools.partial(transition_kernel, phase=phase), in_spec...]
    all_to_all x1, waiting for transfers between devices: 2.13 us -> 0.01 us  [body(): lax.all_to_all(terms, joint, 0, 0, tiled=True, axis_index_groups=Z_GROUPS)]
    all_to_all x1, starting transfers between devices: 9.01 us -> 7.88 us  [body(): lax.all_to_all(band, joint, 0, 0, tiled=True, axis_index_groups=ROW_GROUPS)]
  transfers between devices with their start and end apart: 5 -> 4, of which waited for: 3 -> 0; matrix products, arithmetic and copies ran while one was open for 0% -> 0% of each run, Pallas kernels for 17% -> 18%
where the time goes in v2:
time: 60.8 us; the launch traced here: 60.3 us
  starting transfers between devices  36.4 us (60%)
  Pallas kernels  18.1 us (30%)
  blocking collectives  4.72 us (8%)
  between operations  0.94 us (2%)
    all_to_all x1, starting transfers between devices, body(): lax.all_to_all(terms, joint, 0, 0, tiled=True, axis_index_groups=Z_GROUPS)  12.4 us
    pallas_call x3, Pallas kernels, transition(): pl.pallas_call(functools.partial(transition_kernel, phase=phase), in_spec...  10.6 us
    ppermute x1, starting transfers between devices, body(): cross = lax.ppermute(pack, joint, ends + [(j, i) for i, j in ends])  8.3 us
    all_to_all x1, starting transfers between devices, body(): lax.all_to_all(band, joint, 0, 0, tiled=True, axis_index_groups=ROW_GROUPS)  7.88 us
    all_to_all x1, starting transfers between devices, body(): lax.all_to_all(going, joint, 0, 0, tiled=True, axis_index_groups=PLANE_GR...  7.82 us
    all_gather x1, blocking collectives, body(): lax.all_gather(came, 'row', axis=0, tiled=True, axis_index_groups=CORE_GR...  4.72 us
    pallas_call x1, Pallas kernels, near_diagonal(): pl.pallas_call(band_kernel, in_specs=[HBM] * 6, out_specs=whole(2), out_s...  2.93 us
    pallas_call x1, Pallas kernels, atom_block(): pl.pallas_call(atom_kernel, in_specs=whole(15) + [ANY], out_specs=whole(2...  2.46 us
  transfers between devices with their start and end apart: 4, of which 0 were waited for; matrix products, arithmetic and copies ran while one was open for 0% of the time, Pallas kernels for 18%

profile of v2, /device:TPU:1, one launch (start us, length us, event | category | flops | bytes accessed | tf_op | source)
XLA Modules:
  0.0 60.3 jit_solution(10472268522325148011)
XLA Ops:
  0.7 2.9 %shard_map.212 = (bf16[1024,128]{1,0:T(8,128)(2,1)}, bf16[80,128]{1,0:T(8,128)(2,1)S(1)}) custom-call(bf16[64,128,128]{2,1,0:T(8,128)(2,1)} %given.1, f32[1,128]{1,0:T(1,128)} %bitcast.22, bf16[4,128]{1,0:T(4,128)(2,1)} %bitcast.21, bf16[64,128]{1,0:T(8,128)(2,1)} %atoms.1, s32[1,64]{1,0:T(1,128)} %bitcast.23, s32[1,64]{1,0:T(1,128)} %bitcast.24), custom_call_target="tpu_custom_call" | custom-call | flops 4194304 | bytes 2097152 | tf_op jit(solution)/shard_map/pallas_call | solution.py:382
  3.6 7.9 %all-to-all-start = ((bf16[16,64,128]{2,1,0:T(8,128)(2,1)}), bf16[16,64,128]{2,1,0:T(8,128)(2,1)S(1)}, u32[]{:S(2)}, u32[]{:S(2)}) async-start(bf16[16,64,128]{2,1,0:T(8,128)(2,1)} %bitcast.4), calls=%async_computation | async-start | bytes 524288 | tf_op jit(solution)/shard_map/all_to_all | solution.py:457
  11.5 8.3 %collective-permute-start = (bf16[80,128]{1,0:T(8,128)(2,1)S(1)}, bf16[80,128]{1,0:T(8,128)(2,1)S(1)}, u32[]{:S(2)}, u32[]{:S(2)}) collective-permute-start(bf16[80,128]{1,0:T(8,128)(2,1)S(1)} %get-tuple-element.9._after.pack), channel_id=1, source_target_pairs={{15,16},{31,32},{47,48},{63,64},{79,80},{95,96},{111,112},{127,128... | collective-permute-start | bytes 61448 | tf_op jit(solution)/shard_map/ppermute | solution.py:459
  19.8 0.0 copy-start
  19.8 0.0 copy-start.1
  19.8 0.0 copy-start.2
  19.9 0.0 copy-start.3
  19.9 0.0 copy-start.4
  19.9 0.0 copy-start.5
  19.9 0.0 copy-start.6
  19.9 0.0 copy-start.7
  19.9 0.0 copy-start.8
  19.9 0.0 copy-start.9
  19.9 0.0 copy-start.10
  19.9 0.0 copy-start.11
  20.0 3.7 %shard_map.213._after.given = bf16[64,128,128]{2,1,0:T(8,128)(2,1)S(1)} custom-call(bf16[64,128,128]{2,1,0:T(8,128)(2,1)} %given.1, f32[1,128]{1,0:T(1,128)S(1)} %bitcast.17, bf16[128,1024]{1,0:T(8,128)(2,1)S(1)} %copy-done.12, bf16[512,128]{1,0:T(8,128)(2,1)S(1)} %copy-done.13, bf16[80,128]{1,0:T(8,128)(2,1)S(1)} %get-tuple-element.9._after.pack), custom_call_target="tpu_custom_call" | custom-call | flops 1610612736 | bytes 1048576 | tf_op jit(solution)/shard_map/pallas_call | solution.py:366
  23.8 2.5 %shard_map.214 = (bf16[64,128]{1,0:T(8,128)(2,1)}, bf16[128,128]{1,0:T(8,128)(2,1)}) custom-call(bf16[1024,128]{1,0:T(8,128)(2,1)S(1)} %bitcast.13, bf16[80,128]{1,0:T(8,128)(2,1)S(1)} %collective-permute-done.cross, bf16[80,128]{1,0:T(8,128)(2,1)S(1)} %get-tuple-element.9._after.pack, f32[1,128]{1,0:T(1,128)S(1)} %bitcast.15, ...), custom_call_target="tpu_custom_call" | custom-call | flops 33554432 | bytes 1048576 | tf_op jit(solution)/shard_map/pallas_call | solution.py:413
  26.2 12.4 %all-to-all-start.1 = ((bf16[16,8,128]{2,1,0:T(8,128)(2,1)}), bf16[16,8,128]{2,1,0:T(8,128)(2,1)S(1)}, u32[]{:S(2)}, u32[]{:S(2)}) async-start(bf16[16,8,128]{2,1,0:T(8,128)(2,1)} %bitcast.9), calls=%async_computation.1 | async-start | bytes 65536 | tf_op jit(solution)/shard_map/all_to_all | solution.py:467
  38.7 3.5 %shard_map.215._after.given = bf16[64,128,128]{2,1,0:T(8,128)(2,1)S(1)} custom-call(bf16[64,128,128]{2,1,0:T(8,128)(2,1)S(1)} %shard_map.213._after.given, f32[1,128]{1,0:T(1,128)S(1)} %bitcast.18, bf16[128,1024]{1,0:T(8,128)(2,1)S(1)} %copy-done.12, bf16[512,128]{1,0:T(8,128)(2,1)S(1)} %copy-done.13, ...), custom_call_target="tpu_custom_call", output_to_operand_aliasing={{}: (0, {})} | custom-call | flops 2415919104 | bytes 1572864 | tf_op jit(solution)/shard_map/pallas_call | solution.py:366
  42.2 0.7 %shard_map.216._after = bf16[512,128]{1,0:T(8,128)(2,1)} custom-call(bf16[128,128]{1,0:T(8,128)(2,1)S(1)} %bitcast.14, bf16[64,128,128]{2,1,0:T(8,128)(2,1)S(1)} %shard_map.215._after.given), custom_call_target="tpu_custom_call" | custom-call | tf_op jit(solution)/shard_map/pallas_call | solution.py:427
  42.8 7.8 %all-to-all-start.2 = ((bf16[16,32,128]{2,1,0:T(8,128)(2,1)}), bf16[16,32,128]{2,1,0:T(8,128)(2,1)S(1)}, u32[]{:S(2)}, u32[]{:S(2)}) async-start(bf16[16,32,128]{2,1,0:T(8,128)(2,1)} %bitcast.11), calls=%async_computation.2 | async-start | bytes 262144 | tf_op jit(solution)/shard_map/all_to_all | solution.py:470
  50.7 3.5 %shard_map.217.part = bf16[64,128,128]{2,1,0:T(8,128)(2,1)S(1)} custom-call(bf16[64,128,128]{2,1,0:T(8,128)(2,1)S(1)} %shard_map.215._after.given, f32[1,128]{1,0:T(1,128)S(1)} %bitcast.19, bf16[128,1024]{1,0:T(8,128)(2,1)S(1)} %copy-done.12, bf16[512,128]{1,0:T(8,128)(2,1)S(1)} %copy-done.13, ...), custom_call_target="tpu_custom_call", output_to_operand_aliasing={{}: (0, {})} | custom-call | flops 2415919104 | bytes 1572864 | tf_op jit(solution)/shard_map/pallas_call | solution.py:366
  54.1 4.7 %all_gather.3.came = bf16[1024,128]{1,0:T(8,128)(2,1)S(1)} all-gather(bf16[512,128]{1,0:T(8,128)(2,1)S(1)} %bitcast.20), channel_id=1, replica_groups={{0,16},{32,48},{64,80},{96,112},{128,144},{160,176},{192,208},{224,240}..., dimensions={0}, use_global_device_ids=true | all-gather | bytes 393216 | tf_op jit(solution)/shard_map/all_gather | solution.py:473
  58.9 1.5 %shard_map.218 = bf16[64,128,128]{2,1,0:T(8,128)(2,1)} custom-call(bf16[64,128,128]{2,1,0:T(8,128)(2,1)S(1)} %shard_map.217.part, bf16[1024,128]{1,0:T(8,128)(2,1)S(1)} %all_gather.3.came), custom_call_target="tpu_custom_call" | custom-call | tf_op jit(solution)/shard_map/pallas_call | solution.py:437
  (22 shorter events, 0.0 us)
Async XLA Ops:
  0.6 19.2 %copy-start.13 = (bf16[512,128]{1,0:T(8,128)(2,1)S(1)}, bf16[512,128]{1,0:T(8,128)(2,1)}, u32[]{:S(2)}) copy-start(bf16[512,128]{1,0:T(8,128)(2,1)} %w_down.7) | copy-start | bytes 393220
  0.6 19.2 %copy-start.12 = (bf16[128,1024]{1,0:T(8,128)(2,1)S(1)}, bf16[128,1024]{1,0:T(8,128)(2,1)}, u32[]{:S(2)}) copy-start(bf16[128,1024]{1,0:T(8,128)(2,1)} %w_up.7) | copy-start | bytes 786436
  0.7 19.2 %copy-start.14 = (f32[128]{0:T(128)S(1)}, f32[128]{0:T(128)}, u32[]{:S(2)}) copy-start(f32[128]{0:T(128)} %param.27) | copy-start | bytes 1540
  3.6 20.1 %all-to-all-start = ((bf16[16,64,128]{2,1,0:T(8,128)(2,1)}), bf16[16,64,128]{2,1,0:T(8,128)(2,1)S(1)}, u32[]{:S(2)}, u32[]{:S(2)}) async-start(bf16[16,64,128]{2,1,0:T(8,128)(2,1)} %bitcast.4), calls=%async_computation | async-start | bytes 524288 | tf_op jit(solution)/shard_map/all_to_all | solution.py:457
  11.5 12.2 %collective-permute-start = (bf16[80,128]{1,0:T(8,128)(2,1)S(1)}, bf16[80,128]{1,0:T(8,128)(2,1)S(1)}, u32[]{:S(2)}, u32[]{:S(2)}) collective-permute-start(bf16[80,128]{1,0:T(8,128)(2,1)S(1)} %get-tuple-element.9._after.pack), channel_id=1, source_target_pairs={{15,16},{31,32},{47,48},{63,64},{79,80},{95,96},{111,112},{127,128... | collective-permute-start | bytes 61448 | tf_op jit(solution)/shard_map/ppermute | solution.py:459
  19.8 3.8 %copy-start = (bf16[128,512]{1,0:T(8,128)(2,1)S(1)}, bf16[128,512]{1,0:T(8,128)(2,1)}, u32[]{:S(2)}) copy-start(bf16[128,512]{1,0:T(8,128)(2,1)} %w_up.5) | copy-start | bytes 393220
  19.8 3.8 %copy-start.1 = (bf16[128,384]{1,0:T(8,128)(2,1)S(1)}, bf16[128,384]{1,0:T(8,128)(2,1)}, u32[]{:S(2)}) copy-start(bf16[128,384]{1,0:T(8,128)(2,1)} %w_single.1) | copy-start | bytes 294916
  19.8 3.8 %copy-start.2 = (bf16[384,128]{1,0:T(8,128)(2,1)S(1)}, bf16[384,128]{1,0:T(8,128)(2,1)}, u32[]{:S(2)}) copy-start(bf16[384,128]{1,0:T(8,128)(2,1)} %w_row.1) | copy-start | bytes 294916
  19.9 3.8 %copy-start.3 = (bf16[384,128]{1,0:T(8,128)(2,1)S(1)}, bf16[384,128]{1,0:T(8,128)(2,1)}, u32[]{:S(2)}) copy-start(bf16[384,128]{1,0:T(8,128)(2,1)} %w_col.1) | copy-start | bytes 294916
  19.9 3.8 %copy-start.4 = (bf16[256,128]{1,0:T(8,128)(2,1)S(1)}, bf16[256,128]{1,0:T(8,128)(2,1)}, u32[]{:S(2)}) copy-start(bf16[256,128]{1,0:T(8,128)(2,1)} %w_down.5) | copy-start | bytes 196612
  19.9 3.8 %copy-start.5 = (bf16[128,128]{1,0:T(8,128)(2,1)S(1)}, bf16[128,128]{1,0:T(8,128)(2,1)}, u32[]{:S(2)}) copy-start(bf16[128,128]{1,0:T(8,128)(2,1)} %w_query.1) | copy-start | bytes 98308
  19.9 3.8 %copy-start.6 = (bf16[128,128]{1,0:T(8,128)(2,1)S(1)}, bf16[128,128]{1,0:T(8,128)(2,1)}, u32[]{:S(2)}) copy-start(bf16[128,128]{1,0:T(8,128)(2,1)} %w_key.1) | copy-start | bytes 98308
  19.9 3.8 %copy-start.7 = (bf16[128,128]{1,0:T(8,128)(2,1)S(1)}, bf16[128,128]{1,0:T(8,128)(2,1)}, u32[]{:S(2)}) copy-start(bf16[128,128]{1,0:T(8,128)(2,1)} %w_value.1) | copy-start | bytes 98308
  19.9 3.8 %copy-start.8 = (bf16[128,128]{1,0:T(8,128)(2,1)S(1)}, bf16[128,128]{1,0:T(8,128)(2,1)}, u32[]{:S(2)}) copy-start(bf16[128,128]{1,0:T(8,128)(2,1)} %w_gate.1) | copy-start | bytes 98308
  19.9 3.8 %copy-start.9 = (bf16[128,128]{1,0:T(8,128)(2,1)S(1)}, bf16[128,128]{1,0:T(8,128)(2,1)}, u32[]{:S(2)}) copy-start(bf16[128,128]{1,0:T(8,128)(2,1)} %w_out.1) | copy-start | bytes 98308
  19.9 3.8 %copy-start.10 = (f32[128]{0:T(128)S(1)}, f32[128]{0:T(128)}, u32[]{:S(2)}) copy-start(f32[128]{0:T(128)} %param.30) | copy-start | bytes 1540
  19.9 3.8 %copy-start.11 = (f32[128]{0:T(128)S(1)}, f32[128]{0:T(128)}, u32[]{:S(2)}) copy-start(f32[128]{0:T(128)} %param.36) | copy-start | bytes 1540
  26.2 15.9 %all-to-all-start.1 = ((bf16[16,8,128]{2,1,0:T(8,128)(2,1)}), bf16[16,8,128]{2,1,0:T(8,128)(2,1)S(1)}, u32[]{:S(2)}, u32[]{:S(2)}) async-start(bf16[16,8,128]{2,1,0:T(8,128)(2,1)} %bitcast.9), calls=%async_computation.1 | async-start | bytes 65536 | tf_op jit(solution)/shard_map/all_to_all | solution.py:467
  42.8 11.3 %all-to-all-start.2 = ((bf16[16,32,128]{2,1,0:T(8,128)(2,1)}), bf16[16,32,128]{2,1,0:T(8,128)(2,1)S(1)}, u32[]{:S(2)}, u32[]{:S(2)}) async-start(bf16[16,32,128]{2,1,0:T(8,128)(2,1)} %bitcast.11), calls=%async_computation.2 | async-start | bytes 262144 | tf_op jit(solution)/shard_map/all_to_all | solution.py:470

commit v3 on v2

--- a/solution.py
+++ b/solution.py
@@ -19,7 +19,7 @@
 HEAD = 32
 PACK = 80
 FAR = -3.0e38
-PHASES = (0, 2, 5, 8)
+PHASES = (0, 1, 5, 8)
 PAIR_ROWS = 8
 STEPS = 2
 
@@ -78,16 +78,15 @@
 ):
     row, col = lax.axis_index("row"), lax.axis_index("col")
     offset = 64 * row - 128 * col
-    base = pl.multiple_of(jnp.where(offset >= 64, 48, 0), 16)
     close = (offset >= -64) & (offset <= 128)
-    each = pair.shape[0] // STEPS
+    base = [pl.multiple_of(jnp.clip(offset + 16 * (g - 1), 0, 80), 16) for g in range(4)]
     big = [
         pltpu.make_async_copy(
-            pair.at[pl.ds(each * g, each), pl.ds(base, 80)],
-            tile.at[pl.ds(each * g, each)],
+            pair.at[pl.ds(16 * g, 16), pl.ds(base[g], 48)],
+            tile.at[pl.ds(16 * g, 16)],
             tile_sem.at[g],
         )
-        for g in range(STEPS)
+        for g in range(4)
     ]
 
     @pl.when(close)
@@ -138,14 +137,15 @@
         half = (iota((8, 128), 1) % 32) // 16
         for g in range(STEPS):
             each = 16 // STEPS
-            big[g].wait()
+            for copy in big[4 // STEPS * g : 4 // STEPS * (g + 1)]:
+                copy.wait()
             pieces, inside = [], []
             for k in range(each * g, each * g + each):
                 halves = []
                 for a in range(2):
                     start = offset + 16 * ((k - 1) // 4 + a)
                     inside.append(((start >= 0) & (start <= 112)).astype(jnp.int32))
-                    begin = pl.multiple_of(jnp.clip(start - base, 0, 64), 16)
+                    begin = pl.multiple_of(jnp.clip(start - base[k // 4], 0, 32), 16)
                     halves.append(tile[4 * k : 4 * k + 4, pl.ds(begin, 16), :])
                 pieces.append(jnp.concatenate(halves, axis=1).reshape(128, 128))
             block = jnp.concatenate(pieces, axis=0)
@@ -229,8 +229,7 @@
     scores = jnp.where(states > 0.5, logits + bias, jnp.where(states > -0.5, -1000000000.0, FAR))
     top = jnp.max(scores, axis=-1, keepdims=True)
     expo = jnp.exp(scores - top)
-    weights = (expo / jnp.sum(expo, axis=-1, keepdims=True)).astype(BF16)
-    mixed = dot(weights, value)
+    mixed = dot(expo.astype(BF16), value) / jnp.sum(expo, axis=-1, keepdims=True)
     attended = jnp.zeros((ATOMS, 128), F32)
     for h in range(HEADS):
         attended = jnp.where(head_of == h, mixed[h * ATOMS : (h + 1) * ATOMS, :], attended)
@@ -248,10 +247,10 @@
         (iota((8, 128), 0) % 4).astype(F32) == own_facts[0:1, :], own_facts[1:2, :], 0.0
     )[:, 0:64]
     counts = jnp.sum(chosen, axis=-1, keepdims=True)
-    chosen = chosen.astype(BF16)
     high = single.astype(BF16)
-    low = (single - high.astype(F32)).astype(BF16)
-    singles = ((dot(chosen, high) + dot(chosen, low)) / counts).astype(BF16)
+    parts = jnp.concatenate([high, (single - high.astype(F32)).astype(BF16)], axis=0)
+    twice = jnp.concatenate([chosen, chosen], axis=1).astype(BF16)
+    singles = (dot(twice, parts) / counts).astype(BF16)
     col_terms, row_terms = dot(singles, w_col[...]), dot(singles, w_row[...])
     both = jnp.where(iota((8, 128), 0) < 4, col_terms, row_terms)
     terms[...] = jnp.concatenate([both] * 16, axis=0).astype(BF16)
@@ -267,7 +266,9 @@
         mine = jnp.concatenate([t[4:8] for t in group], axis=0)
         rows = jnp.where(own_zh == zh, mine, rows)
     plane = jnp.concatenate([piece for x in PLANE_ORDER for piece in (cols[x], rows)], axis=0)
-    going[...] = jnp.concatenate([plane] * N4, axis=0).astype(BF16)
+    plane = plane.astype(BF16)
+    for y in range(N4):
+        going[128 * y : 128 * y + 128, :] = plane
 
 
 def transition_kernel(given, gain, w_up, w_down, _after, out, normed, sem, *, phase):
@@ -388,13 +389,13 @@
             jax.ShapeDtypeStruct((PACK, 128), BF16),
         ],
         scratch_shapes=[
-            pltpu.VMEM((64, 80, 128), BF16),
+            pltpu.VMEM((64, 48, 128), BF16),
             pltpu.VMEM((1, 128), F32),
             pltpu.VMEM((4, 128), BF16),
             pltpu.VMEM((64, 128), BF16),
             pltpu.VMEM((1, 64), jnp.int32),
             pltpu.VMEM((1, 64), jnp.int32),
-            pltpu.SemaphoreType.DMA((STEPS,)),
+            pltpu.SemaphoreType.DMA((4,)),
             pltpu.SemaphoreType.DMA((5,)),
         ],
         compiler_params=PARAMS,

time: 60.8 us -> 61.6 us (1.013)
  starting transfers between devices: 36.4 us -> 37.3 us
    all_to_all x1, starting transfers between devices: 12.4 us -> 13.3 us  [body(): lax.all_to_all(terms, joint, 0, 0, tiled=True, axis_index_groups=Z_GROUPS)]
where the time goes in v3:
time: 61.6 us; the launch traced here: 61.2 us
  starting transfers between devices  37.3 us (61%)
  Pallas kernels  18.1 us (29%)
  blocking collectives  4.72 us (8%)
  between operations  0.94 us (2%)
    all_to_all x1, starting transfers between devices, body(): lax.all_to_all(terms, joint, 0, 0, tiled=True, axis_index_groups=Z_GROUPS)  13.3 us
    pallas_call x3, Pallas kernels, transition(): pl.pallas_call(functools.partial(transition_kernel, phase=phase), in_spec...  10.7 us
    ppermute x1, starting transfers between devices, body(): cross = lax.ppermute(pack, joint, ends + [(j, i) for i, j in ends])  8.21 us
    all_to_all x1, starting transfers between devices, body(): lax.all_to_all(band, joint, 0, 0, tiled=True, axis_index_groups=ROW_GROUPS)  7.98 us
    all_to_all x1, starting transfers between devices, body(): lax.all_to_all(going, joint, 0, 0, tiled=True, axis_index_groups=PLANE_GR...  7.81 us
    all_gather x1, blocking collectives, body(): lax.all_gather(came, 'row', axis=0, tiled=True, axis_index_groups=CORE_GR...  4.72 us
    pallas_call x1, Pallas kernels, near_diagonal(): pl.pallas_call(band_kernel, in_specs=[HBM] * 6, out_specs=whole(2), out_s...  2.87 us
    pallas_call x1, Pallas kernels, atom_block(): pl.pallas_call(atom_kernel, in_specs=whole(15) + [ANY], out_specs=whole(2...  2.34 us
  transfers between devices with their start and end apart: 4, of which 0 were waited for; matrix products, arithmetic and copies ran while one was open for 0% of the time, Pallas kernels for 18%

profile of v3, /device:TPU:1, one launch (start us, length us, event | category | flops | bytes accessed | tf_op | source)
XLA Modules:
  0.0 61.2 jit_solution(6280657522893599270)
XLA Ops:
  0.7 2.9 %shard_map.212 = (bf16[1024,128]{1,0:T(8,128)(2,1)}, bf16[80,128]{1,0:T(8,128)(2,1)S(1)}) custom-call(bf16[64,128,128]{2,1,0:T(8,128)(2,1)} %given.1, f32[1,128]{1,0:T(1,128)} %bitcast.22, bf16[4,128]{1,0:T(4,128)(2,1)} %bitcast.21, bf16[64,128]{1,0:T(8,128)(2,1)} %atoms.1, s32[1,64]{1,0:T(1,128)} %bitcast.23, s32[1,64]{1,0:T(1,128)} %bitcast.24), custom_call_target="tpu_custom_call" | custom-call | flops 4194304 | bytes 2097152 | tf_op jit(solution)/shard_map/pallas_call | solution.py:383
  3.5 8.0 %all-to-all-start = ((bf16[16,64,128]{2,1,0:T(8,128)(2,1)}), bf16[16,64,128]{2,1,0:T(8,128)(2,1)S(1)}, u32[]{:S(2)}, u32[]{:S(2)}) async-start(bf16[16,64,128]{2,1,0:T(8,128)(2,1)} %bitcast.4), calls=%async_computation | async-start | bytes 524288 | tf_op jit(solution)/shard_map/all_to_all | solution.py:458
  11.5 8.2 %collective-permute-start = (bf16[80,128]{1,0:T(8,128)(2,1)S(1)}, bf16[80,128]{1,0:T(8,128)(2,1)S(1)}, u32[]{:S(2)}, u32[]{:S(2)}) collective-permute-start(bf16[80,128]{1,0:T(8,128)(2,1)S(1)} %get-tuple-element.9._after.pack), channel_id=1, source_target_pairs={{15,16},{31,32},{47,48},{63,64},{79,80},{95,96},{111,112},{127,128... | collective-permute-start | bytes 61448 | tf_op jit(solution)/shard_map/ppermute | solution.py:460
  19.8 0.0 copy-start.1
  19.8 0.0 copy-start.3
  19.8 0.0 copy-start.4
  19.8 0.0 copy-start.5
  19.8 0.0 copy-start.6
  19.8 0.0 copy-start.7
  19.8 0.0 copy-start.8
  19.8 0.0 copy-start.9
  19.9 0.0 copy-start.10
  19.9 0.0 copy-start.11
  19.9 0.0 copy-start.13
  19.9 0.0 copy-start.14
  19.9 2.8 %shard_map.213._after.given = bf16[64,128,128]{2,1,0:T(8,128)(2,1)S(1)} custom-call(bf16[64,128,128]{2,1,0:T(8,128)(2,1)} %given.1, f32[1,128]{1,0:T(1,128)S(1)} %bitcast.15, bf16[128,1024]{1,0:T(8,128)(2,1)S(1)} %copy-done, bf16[512,128]{1,0:T(8,128)(2,1)S(1)} %copy-done.2, bf16[80,128]{1,0:T(8,128)(2,1)S(1)} %get-tuple-element.9._after.pack), custom_call_target="tpu_custom_call" | custom-call | flops 805306368 | bytes 524288 | tf_op jit(solution)/shard_map/pallas_call | solution.py:367
  22.9 2.3 %shard_map.214 = (bf16[64,128]{1,0:T(8,128)(2,1)}, bf16[128,128]{1,0:T(8,128)(2,1)}) custom-call(bf16[1024,128]{1,0:T(8,128)(2,1)S(1)} %bitcast.13, bf16[80,128]{1,0:T(8,128)(2,1)S(1)} %collective-permute-done.cross, bf16[80,128]{1,0:T(8,128)(2,1)S(1)} %get-tuple-element.9._after.pack, f32[1,128]{1,0:T(1,128)S(1)} %bitcast.18, ...), custom_call_target="tpu_custom_call" | custom-call | flops 33554432 | bytes 1048576 | tf_op jit(solution)/shard_map/pallas_call | solution.py:414
  25.2 13.3 %all-to-all-start.1 = ((bf16[16,8,128]{2,1,0:T(8,128)(2,1)}), bf16[16,8,128]{2,1,0:T(8,128)(2,1)S(1)}, u32[]{:S(2)}, u32[]{:S(2)}) async-start(bf16[16,8,128]{2,1,0:T(8,128)(2,1)} %bitcast.9), calls=%async_computation.1 | async-start | bytes 65536 | tf_op jit(solution)/shard_map/all_to_all | solution.py:468
  38.5 4.5 %shard_map.215._after.given = bf16[64,128,128]{2,1,0:T(8,128)(2,1)S(1)} custom-call(bf16[64,128,128]{2,1,0:T(8,128)(2,1)S(1)} %shard_map.213._after.given, f32[1,128]{1,0:T(1,128)S(1)} %bitcast.16, bf16[128,1024]{1,0:T(8,128)(2,1)S(1)} %copy-done, bf16[512,128]{1,0:T(8,128)(2,1)S(1)} %copy-done.2, ...), custom_call_target="tpu_custom_call", output_to_operand_aliasing={{}: (0, {})} | custom-call | flops 3221225472 | bytes 2097152 | tf_op jit(solution)/shard_map/pallas_call | solution.py:367
  43.0 0.7 %shard_map.216._after = bf16[512,128]{1,0:T(8,128)(2,1)} custom-call(bf16[128,128]{1,0:T(8,128)(2,1)S(1)} %bitcast.14, bf16[64,128,128]{2,1,0:T(8,128)(2,1)S(1)} %shard_map.215._after.given), custom_call_target="tpu_custom_call" | custom-call | tf_op jit(solution)/shard_map/pallas_call | solution.py:428
  43.7 7.8 %all-to-all-start.2 = ((bf16[16,32,128]{2,1,0:T(8,128)(2,1)}), bf16[16,32,128]{2,1,0:T(8,128)(2,1)S(1)}, u32[]{:S(2)}, u32[]{:S(2)}) async-start(bf16[16,32,128]{2,1,0:T(8,128)(2,1)} %bitcast.11), calls=%async_computation.2 | async-start | bytes 262144 | tf_op jit(solution)/shard_map/all_to_all | solution.py:471
  51.5 3.5 %shard_map.217.part = bf16[64,128,128]{2,1,0:T(8,128)(2,1)S(1)} custom-call(bf16[64,128,128]{2,1,0:T(8,128)(2,1)S(1)} %shard_map.215._after.given, f32[1,128]{1,0:T(1,128)S(1)} %bitcast.17, bf16[128,1024]{1,0:T(8,128)(2,1)S(1)} %copy-done, bf16[512,128]{1,0:T(8,128)(2,1)S(1)} %copy-done.2, ...), custom_call_target="tpu_custom_call", output_to_operand_aliasing={{}: (0, {})} | custom-call | flops 2415919104 | bytes 1572864 | tf_op jit(solution)/shard_map/pallas_call | solution.py:367
  55.0 4.7 %all_gather.3.came = bf16[1024,128]{1,0:T(8,128)(2,1)S(1)} all-gather(bf16[512,128]{1,0:T(8,128)(2,1)S(1)} %bitcast.20), channel_id=1, replica_groups={{0,16},{32,48},{64,80},{96,112},{128,144},{160,176},{192,208},{224,240}..., dimensions={0}, use_global_device_ids=true | all-gather | bytes 393216 | tf_op jit(solution)/shard_map/all_gather | solution.py:474
  59.7 1.5 %shard_map.218 = bf16[64,128,128]{2,1,0:T(8,128)(2,1)} custom-call(bf16[64,128,128]{2,1,0:T(8,128)(2,1)S(1)} %shard_map.217.part, bf16[1024,128]{1,0:T(8,128)(2,1)S(1)} %all_gather.3.came), custom_call_target="tpu_custom_call" | custom-call | tf_op jit(solution)/shard_map/pallas_call | solution.py:438
  (22 shorter events, 0.0 us)
Async XLA Ops:
  0.6 19.1 %copy-start.2 = (bf16[512,128]{1,0:T(8,128)(2,1)S(1)}, bf16[512,128]{1,0:T(8,128)(2,1)}, u32[]{:S(2)}) copy-start(bf16[512,128]{1,0:T(8,128)(2,1)} %w_down.7) | copy-start | bytes 393220
  0.6 19.1 %copy-start = (bf16[128,1024]{1,0:T(8,128)(2,1)S(1)}, bf16[128,1024]{1,0:T(8,128)(2,1)}, u32[]{:S(2)}) copy-start(bf16[128,1024]{1,0:T(8,128)(2,1)} %w_up.7) | copy-start | bytes 786436
  0.7 19.1 %copy-start.12 = (f32[128]{0:T(128)S(1)}, f32[128]{0:T(128)}, u32[]{:S(2)}) copy-start(f32[128]{0:T(128)} %param.27) | copy-start | bytes 1540
  3.5 19.2 %all-to-all-start = ((bf16[16,64,128]{2,1,0:T(8,128)(2,1)}), bf16[16,64,128]{2,1,0:T(8,128)(2,1)S(1)}, u32[]{:S(2)}, u32[]{:S(2)}) async-start(bf16[16,64,128]{2,1,0:T(8,128)(2,1)} %bitcast.4), calls=%async_computation | async-start | bytes 524288 | tf_op jit(solution)/shard_map/all_to_all | solution.py:458
  11.5 11.2 %collective-permute-start = (bf16[80,128]{1,0:T(8,128)(2,1)S(1)}, bf16[80,128]{1,0:T(8,128)(2,1)S(1)}, u32[]{:S(2)}, u32[]{:S(2)}) collective-permute-start(bf16[80,128]{1,0:T(8,128)(2,1)S(1)} %get-tuple-element.9._after.pack), channel_id=1, source_target_pairs={{15,16},{31,32},{47,48},{63,64},{79,80},{95,96},{111,112},{127,128... | collective-permute-start | bytes 61448 | tf_op jit(solution)/shard_map/ppermute | solution.py:460
  19.8 3.0 %copy-start.1 = (bf16[128,512]{1,0:T(8,128)(2,1)S(1)}, bf16[128,512]{1,0:T(8,128)(2,1)}, u32[]{:S(2)}) copy-start(bf16[128,512]{1,0:T(8,128)(2,1)} %w_up.5) | copy-start | bytes 393220
  19.8 3.0 %copy-start.3 = (bf16[128,384]{1,0:T(8,128)(2,1)S(1)}, bf16[128,384]{1,0:T(8,128)(2,1)}, u32[]{:S(2)}) copy-start(bf16[128,384]{1,0:T(8,128)(2,1)} %w_single.1) | copy-start | bytes 294916
  19.8 3.0 %copy-start.4 = (bf16[384,128]{1,0:T(8,128)(2,1)S(1)}, bf16[384,128]{1,0:T(8,128)(2,1)}, u32[]{:S(2)}) copy-start(bf16[384,128]{1,0:T(8,128)(2,1)} %w_row.1) | copy-start | bytes 294916
  19.8 3.0 %copy-start.5 = (bf16[384,128]{1,0:T(8,128)(2,1)S(1)}, bf16[384,128]{1,0:T(8,128)(2,1)}, u32[]{:S(2)}) copy-start(bf16[384,128]{1,0:T(8,128)(2,1)} %w_col.1) | copy-start | bytes 294916
  19.8 3.0 %copy-start.6 = (bf16[256,128]{1,0:T(8,128)(2,1)S(1)}, bf16[256,128]{1,0:T(8,128)(2,1)}, u32[]{:S(2)}) copy-start(bf16[256,128]{1,0:T(8,128)(2,1)} %w_down.5) | copy-start | bytes 196612
  19.8 3.0 %copy-start.7 = (bf16[128,128]{1,0:T(8,128)(2,1)S(1)}, bf16[128,128]{1,0:T(8,128)(2,1)}, u32[]{:S(2)}) copy-start(bf16[128,128]{1,0:T(8,128)(2,1)} %w_query.1) | copy-start | bytes 98308
  19.8 3.0 %copy-start.8 = (bf16[128,128]{1,0:T(8,128)(2,1)S(1)}, bf16[128,128]{1,0:T(8,128)(2,1)}, u32[]{:S(2)}) copy-start(bf16[128,128]{1,0:T(8,128)(2,1)} %w_key.1) | copy-start | bytes 98308
  19.8 3.0 %copy-start.9 = (bf16[128,128]{1,0:T(8,128)(2,1)S(1)}, bf16[128,128]{1,0:T(8,128)(2,1)}, u32[]{:S(2)}) copy-start(bf16[128,128]{1,0:T(8,128)(2,1)} %w_value.1) | copy-start | bytes 98308
  19.9 3.0 %copy-start.10 = (bf16[128,128]{1,0:T(8,128)(2,1)S(1)}, bf16[128,128]{1,0:T(8,128)(2,1)}, u32[]{:S(2)}) copy-start(bf16[128,128]{1,0:T(8,128)(2,1)} %w_gate.1) | copy-start | bytes 98308
  19.9 3.0 %copy-start.11 = (bf16[128,128]{1,0:T(8,128)(2,1)S(1)}, bf16[128,128]{1,0:T(8,128)(2,1)}, u32[]{:S(2)}) copy-start(bf16[128,128]{1,0:T(8,128)(2,1)} %w_out.1) | copy-start | bytes 98308
  19.9 3.0 %copy-start.13 = (f32[128]{0:T(128)S(1)}, f32[128]{0:T(128)}, u32[]{:S(2)}) copy-start(f32[128]{0:T(128)} %param.30) | copy-start | bytes 1540
  19.9 3.0 %copy-start.14 = (f32[128]{0:T(128)S(1)}, f32[128]{0:T(128)}, u32[]{:S(2)}) copy-start(f32[128]{0:T(128)} %param.36) | copy-start | bytes 1540
  25.2 17.8 %all-to-all-start.1 = ((bf16[16,8,128]{2,1,0:T(8,128)(2,1)}), bf16[16,8,128]{2,1,0:T(8,128)(2,1)S(1)}, u32[]{:S(2)}, u32[]{:S(2)}) async-start(bf16[16,8,128]{2,1,0:T(8,128)(2,1)} %bitcast.9), calls=%async_computation.1 | async-start | bytes 65536 | tf_op jit(solution)/shard_map/all_to_all | solution.py:468
  43.7 11.3 %all-to-all-start.2 = ((bf16[16,32,128]{2,1,0:T(8,128)(2,1)}), bf16[16,32,128]{2,1,0:T(8,128)(2,1)S(1)}, u32[]{:S(2)}, u32[]{:S(2)}) async-start(bf16[16,32,128]{2,1,0:T(8,128)(2,1)} %bitcast.11), calls=%async_computation.2 | async-start | bytes 262144 | tf_op jit(solution)/shard_map/all_to_all | solution.py:471

commit v4 on v3

--- a/solution.py
+++ b/solution.py
@@ -19,7 +19,7 @@
 HEAD = 32
 PACK = 80
 FAR = -3.0e38
-PHASES = (0, 1, 5, 8)
+PHASES = (0, 2, 5, 8)
 PAIR_ROWS = 8
 STEPS = 2
 
@@ -28,8 +28,8 @@
     return ((y * N4 + zh) * 2 + core) * 16 + zl * N4 + x
 
 
-Z_ORDER = ((2, 0),) + tuple(
-    (zh, zl) for zh in (0, 1, 3, 2) for zl in range(N4) if (zh, zl) != (2, 0)
+Z_ORDER = ((2, 1),) + tuple(
+    (zh, zl) for zh in (0, 1, 3, 2) for zl in range(N4) if (zh, zl) != (2, 1)
 )
 PLANE_ORDER = (3, 0, 1, 2)
 Z_GROUPS = [

time: 61.6 us -> 60.1 us (0.976)
  starting transfers between devices: 37.3 us -> 35.2 us
    all_to_all x1, starting transfers between devices: 7.81 us -> 6.66 us  [body(): lax.all_to_all(going, joint, 0, 0, tiled=True, axis_index_groups=PLANE_GR...]
    all_to_all x1, starting transfers between devices: 13.3 us -> 12.3 us  [body(): lax.all_to_all(terms, joint, 0, 0, tiled=True, axis_index_groups=Z_GROUPS)]
  transfers between devices with their start and end apart: 4 -> 4, of which waited for: 0 -> 1; matrix products, arithmetic and copies ran while one was open for 0% -> 0% of each run, Pallas kernels for 18% -> 18%
where the time goes in v4:
time: 60.1 us; the launch traced here: 59.7 us
  starting transfers between devices  35.2 us (59%)
  Pallas kernels  17.9 us (30%)
  blocking collectives  5.1 us (8%)
  between operations  0.94 us (2%)
    all_to_all x1, starting transfers between devices, body(): lax.all_to_all(terms, joint, 0, 0, tiled=True, axis_index_groups=Z_GROUPS)  12.3 us
    pallas_call x3, Pallas kernels, transition(): pl.pallas_call(functools.partial(transition_kernel, phase=phase), in_spec...  10.6 us
    ppermute x1, starting transfers between devices, body(): cross = lax.ppermute(pack, joint, ends + [(j, i) for i, j in ends])  8.21 us
    all_to_all x1, starting transfers between devices, body(): lax.all_to_all(band, joint, 0, 0, tiled=True, axis_index_groups=ROW_GROUPS)  7.98 us
    all_to_all x1, starting transfers between devices, body(): lax.all_to_all(going, joint, 0, 0, tiled=True, axis_index_groups=PLANE_GR...  6.66 us
    all_gather x1, blocking collectives, body(): lax.all_gather(came, 'row', axis=0, tiled=True, axis_index_groups=CORE_GR...  5.1 us
    pallas_call x1, Pallas kernels, near_diagonal(): pl.pallas_call(band_kernel, in_specs=[HBM] * 6, out_specs=whole(2), out_s...  2.87 us
    pallas_call x1, Pallas kernels, atom_block(): pl.pallas_call(atom_kernel, in_specs=whole(15) + [ANY], out_specs=whole(2...  2.33 us
  transfers between devices with their start and end apart: 4, of which 1 were waited for; matrix products, arithmetic and copies ran while one was open for 0% of the time, Pallas kernels for 18%

profile of v4, /device:TPU:1, one launch (start us, length us, event | category | flops | bytes accessed | tf_op | source)
XLA Modules:
  0.0 59.7 jit_solution(18094472544652767942)
XLA Ops:
  0.7 2.9 %shard_map.212 = (bf16[1024,128]{1,0:T(8,128)(2,1)}, bf16[80,128]{1,0:T(8,128)(2,1)S(1)}) custom-call(bf16[64,128,128]{2,1,0:T(8,128)(2,1)} %given.1, f32[1,128]{1,0:T(1,128)} %bitcast.22, bf16[4,128]{1,0:T(4,128)(2,1)} %bitcast.21, bf16[64,128]{1,0:T(8,128)(2,1)} %atoms.1, s32[1,64]{1,0:T(1,128)} %bitcast.23, s32[1,64]{1,0:T(1,128)} %bitcast.24), custom_call_target="tpu_custom_call" | custom-call | flops 4194304 | bytes 2097152 | tf_op jit(solution)/shard_map/pallas_call | solution.py:383
  3.5 8.0 %all-to-all-start = ((bf16[16,64,128]{2,1,0:T(8,128)(2,1)}), bf16[16,64,128]{2,1,0:T(8,128)(2,1)S(1)}, u32[]{:S(2)}, u32[]{:S(2)}) async-start(bf16[16,64,128]{2,1,0:T(8,128)(2,1)} %bitcast.4), calls=%async_computation | async-start | bytes 524288 | tf_op jit(solution)/shard_map/all_to_all | solution.py:458
  11.5 8.2 %collective-permute-start = (bf16[80,128]{1,0:T(8,128)(2,1)S(1)}, bf16[80,128]{1,0:T(8,128)(2,1)S(1)}, u32[]{:S(2)}, u32[]{:S(2)}) collective-permute-start(bf16[80,128]{1,0:T(8,128)(2,1)S(1)} %get-tuple-element.9._after.pack), channel_id=1, source_target_pairs={{15,16},{31,32},{47,48},{63,64},{79,80},{95,96},{111,112},{127,128... | collective-permute-start | bytes 61448 | tf_op jit(solution)/shard_map/ppermute | solution.py:460
  19.8 0.0 copy-start
  19.8 0.0 copy-start.1
  19.8 0.0 copy-start.2
  19.8 0.0 copy-start.3
  19.8 0.0 copy-start.4
  19.8 0.0 copy-start.5
  19.8 0.0 copy-start.6
  19.8 0.0 copy-start.7
  19.9 0.0 copy-start.8
  19.9 0.0 copy-start.10
  19.9 0.0 copy-start.11
  19.9 3.7 %shard_map.213._after.given = bf16[64,128,128]{2,1,0:T(8,128)(2,1)S(1)} custom-call(bf16[64,128,128]{2,1,0:T(8,128)(2,1)} %given.1, f32[1,128]{1,0:T(1,128)S(1)} %bitcast.17, bf16[128,1024]{1,0:T(8,128)(2,1)S(1)} %copy-done.12, bf16[512,128]{1,0:T(8,128)(2,1)S(1)} %copy-done.13, bf16[80,128]{1,0:T(8,128)(2,1)S(1)} %get-tuple-element.9._after.pack), custom_call_target="tpu_custom_call" | custom-call | flops 1610612736 | bytes 1048576 | tf_op jit(solution)/shard_map/pallas_call | solution.py:367
  23.7 2.3 %shard_map.214 = (bf16[64,128]{1,0:T(8,128)(2,1)}, bf16[128,128]{1,0:T(8,128)(2,1)}) custom-call(bf16[1024,128]{1,0:T(8,128)(2,1)S(1)} %bitcast.13, bf16[80,128]{1,0:T(8,128)(2,1)S(1)} %collective-permute-done.cross, bf16[80,128]{1,0:T(8,128)(2,1)S(1)} %get-tuple-element.9._after.pack, f32[1,128]{1,0:T(1,128)S(1)} %bitcast.15, ...), custom_call_target="tpu_custom_call" | custom-call | flops 33554432 | bytes 1048576 | tf_op jit(solution)/shard_map/pallas_call | solution.py:414
  26.0 12.3 %all-to-all-start.1 = ((bf16[16,8,128]{2,1,0:T(8,128)(2,1)}), bf16[16,8,128]{2,1,0:T(8,128)(2,1)S(1)}, u32[]{:S(2)}, u32[]{:S(2)}) async-start(bf16[16,8,128]{2,1,0:T(8,128)(2,1)} %bitcast.9), calls=%async_computation.1 | async-start | bytes 65536 | tf_op jit(solution)/shard_map/all_to_all | solution.py:468
  38.4 3.5 %shard_map.215._after.given = bf16[64,128,128]{2,1,0:T(8,128)(2,1)S(1)} custom-call(bf16[64,128,128]{2,1,0:T(8,128)(2,1)S(1)} %shard_map.213._after.given, f32[1,128]{1,0:T(1,128)S(1)} %bitcast.18, bf16[128,1024]{1,0:T(8,128)(2,1)S(1)} %copy-done.12, bf16[512,128]{1,0:T(8,128)(2,1)S(1)} %copy-done.13, ...), custom_call_target="tpu_custom_call", output_to_operand_aliasing={{}: (0, {})} | custom-call | flops 2415919104 | bytes 1572864 | tf_op jit(solution)/shard_map/pallas_call | solution.py:367
  41.8 0.4 all-to-all-done.1
  42.3 0.7 %shard_map.216._after = bf16[512,128]{1,0:T(8,128)(2,1)} custom-call(bf16[128,128]{1,0:T(8,128)(2,1)S(1)} %bitcast.14, bf16[64,128,128]{2,1,0:T(8,128)(2,1)S(1)} %shard_map.215._after.given), custom_call_target="tpu_custom_call" | custom-call | tf_op jit(solution)/shard_map/pallas_call | solution.py:428
  43.0 6.7 %all-to-all-start.2 = ((bf16[16,32,128]{2,1,0:T(8,128)(2,1)}), bf16[16,32,128]{2,1,0:T(8,128)(2,1)S(1)}, u32[]{:S(2)}, u32[]{:S(2)}) async-start(bf16[16,32,128]{2,1,0:T(8,128)(2,1)} %bitcast.11), calls=%async_computation.2 | async-start | bytes 262144 | tf_op jit(solution)/shard_map/all_to_all | solution.py:471
  49.6 3.5 %shard_map.217.part = bf16[64,128,128]{2,1,0:T(8,128)(2,1)S(1)} custom-call(bf16[64,128,128]{2,1,0:T(8,128)(2,1)S(1)} %shard_map.215._after.given, f32[1,128]{1,0:T(1,128)S(1)} %bitcast.19, bf16[128,1024]{1,0:T(8,128)(2,1)S(1)} %copy-done.12, bf16[512,128]{1,0:T(8,128)(2,1)S(1)} %copy-done.13, ...), custom_call_target="tpu_custom_call", output_to_operand_aliasing={{}: (0, {})} | custom-call | flops 2415919104 | bytes 1572864 | tf_op jit(solution)/shard_map/pallas_call | solution.py:367
  53.1 5.1 %all_gather.3.came = bf16[1024,128]{1,0:T(8,128)(2,1)S(1)} all-gather(bf16[512,128]{1,0:T(8,128)(2,1)S(1)} %bitcast.20), channel_id=1, replica_groups={{0,16},{32,48},{64,80},{96,112},{128,144},{160,176},{192,208},{224,240}..., dimensions={0}, use_global_device_ids=true | all-gather | bytes 393216 | tf_op jit(solution)/shard_map/all_gather | solution.py:474
  58.2 1.5 %shard_map.218 = bf16[64,128,128]{2,1,0:T(8,128)(2,1)} custom-call(bf16[64,128,128]{2,1,0:T(8,128)(2,1)S(1)} %shard_map.217.part, bf16[1024,128]{1,0:T(8,128)(2,1)S(1)} %all_gather.3.came), custom_call_target="tpu_custom_call" | custom-call | tf_op jit(solution)/shard_map/pallas_call | solution.py:438
  (22 shorter events, 0.0 us)
Async XLA Ops:
  0.6 19.1 %copy-start.13 = (bf16[512,128]{1,0:T(8,128)(2,1)S(1)}, bf16[512,128]{1,0:T(8,128)(2,1)}, u32[]{:S(2)}) copy-start(bf16[512,128]{1,0:T(8,128)(2,1)} %w_down.7) | copy-start | bytes 393220
  0.6 19.1 %copy-start.12 = (bf16[128,1024]{1,0:T(8,128)(2,1)S(1)}, bf16[128,1024]{1,0:T(8,128)(2,1)}, u32[]{:S(2)}) copy-start(bf16[128,1024]{1,0:T(8,128)(2,1)} %w_up.7) | copy-start | bytes 786436
  0.7 19.1 %copy-start.14 = (f32[128]{0:T(128)S(1)}, f32[128]{0:T(128)}, u32[]{:S(2)}) copy-start(f32[128]{0:T(128)} %param.27) | copy-start | bytes 1540
  3.5 20.0 %all-to-all-start = ((bf16[16,64,128]{2,1,0:T(8,128)(2,1)}), bf16[16,64,128]{2,1,0:T(8,128)(2,1)S(1)}, u32[]{:S(2)}, u32[]{:S(2)}) async-start(bf16[16,64,128]{2,1,0:T(8,128)(2,1)} %bitcast.4), calls=%async_computation | async-start | bytes 524288 | tf_op jit(solution)/shard_map/all_to_all | solution.py:458
  11.5 12.1 %collective-permute-start = (bf16[80,128]{1,0:T(8,128)(2,1)S(1)}, bf16[80,128]{1,0:T(8,128)(2,1)S(1)}, u32[]{:S(2)}, u32[]{:S(2)}) collective-permute-start(bf16[80,128]{1,0:T(8,128)(2,1)S(1)} %get-tuple-element.9._after.pack), channel_id=1, source_target_pairs={{15,16},{31,32},{47,48},{63,64},{79,80},{95,96},{111,112},{127,128... | collective-permute-start | bytes 61448 | tf_op jit(solution)/shard_map/ppermute | solution.py:460
  19.8 3.8 %copy-start = (bf16[128,512]{1,0:T(8,128)(2,1)S(1)}, bf16[128,512]{1,0:T(8,128)(2,1)}, u32[]{:S(2)}) copy-start(bf16[128,512]{1,0:T(8,128)(2,1)} %w_up.5) | copy-start | bytes 393220
  19.8 3.8 %copy-start.1 = (bf16[128,384]{1,0:T(8,128)(2,1)S(1)}, bf16[128,384]{1,0:T(8,128)(2,1)}, u32[]{:S(2)}) copy-start(bf16[128,384]{1,0:T(8,128)(2,1)} %w_single.1) | copy-start | bytes 294916
  19.8 3.8 %copy-start.2 = (bf16[384,128]{1,0:T(8,128)(2,1)S(1)}, bf16[384,128]{1,0:T(8,128)(2,1)}, u32[]{:S(2)}) copy-start(bf16[384,128]{1,0:T(8,128)(2,1)} %w_row.1) | copy-start | bytes 294916
  19.8 3.8 %copy-start.3 = (bf16[384,128]{1,0:T(8,128)(2,1)S(1)}, bf16[384,128]{1,0:T(8,128)(2,1)}, u32[]{:S(2)}) copy-start(bf16[384,128]{1,0:T(8,128)(2,1)} %w_col.1) | copy-start | bytes 294916
  19.8 3.8 %copy-start.4 = (bf16[256,128]{1,0:T(8,128)(2,1)S(1)}, bf16[256,128]{1,0:T(8,128)(2,1)}, u32[]{:S(2)}) copy-start(bf16[256,128]{1,0:T(8,128)(2,1)} %w_down.5) | copy-start | bytes 196612
  19.8 3.8 %copy-start.5 = (bf16[128,128]{1,0:T(8,128)(2,1)S(1)}, bf16[128,128]{1,0:T(8,128)(2,1)}, u32[]{:S(2)}) copy-start(bf16[128,128]{1,0:T(8,128)(2,1)} %w_query.1) | copy-start | bytes 98308
  19.8 3.8 %copy-start.6 = (bf16[128,128]{1,0:T(8,128)(2,1)S(1)}, bf16[128,128]{1,0:T(8,128)(2,1)}, u32[]{:S(2)}) copy-start(bf16[128,128]{1,0:T(8,128)(2,1)} %w_key.1) | copy-start | bytes 98308
  19.8 3.8 %copy-start.7 = (bf16[128,128]{1,0:T(8,128)(2,1)S(1)}, bf16[128,128]{1,0:T(8,128)(2,1)}, u32[]{:S(2)}) copy-start(bf16[128,128]{1,0:T(8,128)(2,1)} %w_value.1) | copy-start | bytes 98308
  19.9 3.8 %copy-start.8 = (bf16[128,128]{1,0:T(8,128)(2,1)S(1)}, bf16[128,128]{1,0:T(8,128)(2,1)}, u32[]{:S(2)}) copy-start(bf16[128,128]{1,0:T(8,128)(2,1)} %w_gate.1) | copy-start | bytes 98308
  19.9 3.8 %copy-start.9 = (bf16[128,128]{1,0:T(8,128)(2,1)S(1)}, bf16[128,128]{1,0:T(8,128)(2,1)}, u32[]{:S(2)}) copy-start(bf16[128,128]{1,0:T(8,128)(2,1)} %w_out.1) | copy-start | bytes 98308
  19.9 3.8 %copy-start.10 = (f32[128]{0:T(128)S(1)}, f32[128]{0:T(128)}, u32[]{:S(2)}) copy-start(f32[128]{0:T(128)} %param.30) | copy-start | bytes 1540
  19.9 3.8 %copy-start.11 = (f32[128]{0:T(128)S(1)}, f32[128]{0:T(128)}, u32[]{:S(2)}) copy-start(f32[128]{0:T(128)} %param.36) | copy-start | bytes 1540
  26.0 16.2 %all-to-all-start.1 = ((bf16[16,8,128]{2,1,0:T(8,128)(2,1)}), bf16[16,8,128]{2,1,0:T(8,128)(2,1)S(1)}, u32[]{:S(2)}, u32[]{:S(2)}) async-start(bf16[16,8,128]{2,1,0:T(8,128)(2,1)} %bitcast.9), calls=%async_computation.1 | async-start | bytes 65536 | tf_op jit(solution)/shard_map/all_to_all | solution.py:468
  43.0 10.1 %all-to-all-start.2 = ((bf16[16,32,128]{2,1,0:T(8,128)(2,1)}), bf16[16,32,128]{2,1,0:T(8,128)(2,1)S(1)}, u32[]{:S(2)}, u32[]{:S(2)}) async-start(bf16[16,32,128]{2,1,0:T(8,128)(2,1)} %bitcast.11), calls=%async_computation.2 | async-start | bytes 262144 | tf_op jit(solution)/shard_map/all_to_all | solution.py:471
